TPU v7x, 512 devices: a whole 4x8x8 slice. The times are simulated.
512 devices in a mesh: ctx: 64 (over x, z, core), head: 8 (over y).
Axes of the slice: x: 4, y: 8, z: 8, core: 2. Of those that a mesh axis runs over, the one named last changes fastest.
Arguments:
- hidden: bfloat16 [16384, 4096], P('ctx'), may hold values from -6 to 6
- w_bc: bfloat16 [4096, 2048], P('ctx', 'head'), may hold values from -0.0078125 to 0.0078125
- x_act: bfloat16 [16384, 4096], P('ctx', 'head'), may hold values from -6 to 6
- step_size: float32 [64, 16384], P('head', 'ctx'), may hold values from 0.5 to 1.5
- decay_rate: float32 [64], P('head'), may hold values from 2.4414063e-05 to 0.04
- skip_gain: float32 [64], P('head'), may hold values from 0.5 to 1.5
- logp_dir: bfloat16 [16384, 4096], P('ctx', 'head'), may hold values from -0.29882812 to 0.29882812
- base_logp: float32 [16384], P('ctx'), may hold values from -6 to 6
- seq_stretches: int32 [4], replicated, may hold values from 1 to 32, 64 in all
- resp_mask: int32 [16384], P('ctx'), may hold values 0 or 1
Outputs:
- grad_x: bfloat16 [16384, 4096], P('ctx', 'head')
- grad_step: float32 [64, 16384], P('head', 'ctx')
- grad_rate: float32 [64], P('head')
- grad_skip: float32 [64], P('head')
- grad_w: float32 [4096, 2048], P('ctx', 'head')
Inputs may be any that keep to these rules, and one draw needn't show every extreme that they name: Sequences 2p and 2p+1 are pair p's chosen and rejected answers; sequence j holds seq_stretches[j] whole blocks of 256 tokens, and the blocks of all 4 sequences add up to 64; some sequence has exactly 32 blocks.
All inputs are finite; a program needn't handle non-finite values. No bound on the sum of `resp_mask` on one device may be relied on, other than what follows from the above.
Results may differ from a plain program's by a relative error of at most 0.015.
Values may be sent and summed in bfloat16 or wider, within the bound.
A program may use at most 64 MiB of HBM per device.

v0:
```python
import jax
import jax.numpy as jnp
from jax import lax
from jax.sharding import PartitionSpec as P

HEADDIM = 64
NSTATE = 128


hinge_sharp = 0.005
hinge_margin = 10.0


def prefix(x, axis, combine, identity, reverse):
    size, index = (lax.axis_size(axis), lax.axis_index(axis))
    everything = jax.tree.map(lambda part: lax.all_gather(part, axis), x)
    start = jax.tree.map(
        lambda part, zero: jnp.broadcast_to(jnp.asarray(zero, part.dtype), part.shape), x, identity
    )

    def hop(k, before):
        at = size - 1 - k if reverse else k
        reached = at > index if reverse else at < index
        new = combine(before, jax.tree.map(lambda part: part[at], everything))
        return jax.tree.map(lambda a, b: jnp.where(reached, a, b), new, before)

    return lax.fori_loop(0, size, hop, start)


def einsum_wide(form, left, right):
    return jnp.einsum(form, left, right, preferred_element_type=jnp.float32)


def block_state(inputs, step_group, rate_group, b_input):
    cum_decay = jnp.cumsum(-step_group * rate_group[:, :, None], axis=2)
    last_cum = cum_decay[:, :, -1:]
    factor = jnp.exp(last_cum - cum_decay) * step_group
    b_float = b_input.astype(jnp.float32).transpose(1, 0, 2)
    weighted = (factor[:, :, :, None] * b_float[:, None]).astype(jnp.bfloat16)
    local_state = einsum_wide("tghp,ghtn->ghpn", inputs, weighted)
    block_decay = jnp.exp(last_cum[:, :, 0])
    return (local_state, block_decay, cum_decay)


def block_output(inputs, step_group, cum_decay, skip_group, b_input, c_input, state_in):
    length = inputs.shape[0]
    scores = einsum_wide("tgn,sgn->gts", c_input, b_input)
    row_index = lax.broadcasted_iota(jnp.int32, (length, length), 0)
    col_index = lax.broadcasted_iota(jnp.int32, (length, length), 1)
    causal = row_index >= col_index
    gap_decay = jnp.where(causal, cum_decay[:, :, :, None] - cum_decay[:, :, None, :], 0.0)
    weights = jnp.where(
        causal, jnp.exp(gap_decay) * scores[:, None] * step_group[:, :, None, :], 0.0
    )
    weights = weights.astype(jnp.bfloat16)
    within = einsum_wide("ghts,sghp->tghp", weights, inputs)
    carried = jnp.einsum(
        "tgn,ghpn->tghp", c_input.astype(jnp.float32), state_in, precision=lax.Precision.HIGHEST
    )
    across = carried * jnp.exp(cum_decay).transpose(2, 0, 1)[:, :, :, None]
    return within + across + skip_group[None, :, :, None] * inputs.astype(jnp.float32)


def chain_pair(earlier, later_part):
    return (
        earlier[0] * later_part[0],
        later_part[0][:, :, None, None] * earlier[1] + later_part[1],
    )


def forward_carry(element):
    identity = (jnp.ones_like(element[0]), jnp.zeros_like(element[1]))
    return prefix(element, "ctx", chain_pair, identity, False)[1]


def reverse_carry(element):
    identity = (jnp.ones_like(element[0]), jnp.zeros_like(element[1]))
    return prefix(element, "ctx", chain_pair, identity, True)[1]


def body(
    hidden,
    w_bc,
    x_act,
    step_size,
    decay_rate,
    skip_gain,
    logp_dir,
    base_logp,
    seq_stretches,
    resp_mask,
):
    tok_count = x_act.shape[0]
    head_count = step_size.shape[0]
    column_count = w_bc.shape[1]
    group_count = column_count // (2 * NSTATE)
    per_group = head_count // group_count
    ctx_index = lax.axis_index("ctx")
    head_index = lax.axis_index("head")
    columns = hidden
    projected = jnp.dot(
        columns, lax.all_gather(w_bc, "ctx", axis=0, tiled=True), preferred_element_type=jnp.float32
    )
    projected = projected.astype(jnp.bfloat16).reshape(tok_count, group_count, 2, NSTATE)
    b_input = projected[:, :, 0]
    c_input = projected[:, :, 1]
    seq_ends = jnp.cumsum(seq_stretches)
    seq_starts = seq_ends - seq_stretches
    my_seq = jnp.sum((seq_starts <= ctx_index).astype(jnp.int32)) - 1
    keep_forward = 1.0 - jnp.any(seq_starts == ctx_index + 1).astype(jnp.float32)
    keep_reverse = 1.0 - jnp.any(seq_starts == ctx_index).astype(jnp.float32)
    inputs = x_act.reshape(tok_count, group_count, per_group, HEADDIM)
    step_group = step_size.reshape(group_count, per_group, tok_count)
    rate_group = decay_rate.reshape(group_count, per_group)
    skip_group = skip_gain.reshape(group_count, per_group)
    (local_state, block_decay, cum_decay), pull_state = jax.vjp(
        block_state, inputs, step_group, rate_group, b_input
    )
    directions = logp_dir.reshape(tok_count, group_count, per_group, HEADDIM).astype(jnp.float32)
    mask_float = resp_mask.astype(jnp.float32)
    growth = jnp.exp(cum_decay).transpose(2, 0, 1)[:, :, :, None]
    c_float = c_input.astype(jnp.float32)
    state_in = forward_carry((block_decay * keep_forward, local_state * keep_forward))
    outputs, pull_output = jax.vjp(
        block_output, inputs, step_group, cum_decay, skip_group, b_input, c_input, state_in
    )
    own_sum = jnp.sum(mask_float * jnp.sum(directions * outputs, axis=(1, 2, 3)))
    own_sum = own_sum + jnp.where(head_index == 0, jnp.sum(mask_float * base_logp), 0.0)
    seq_count = seq_stretches.shape[0]
    seq_onehot = (jnp.arange(seq_count, dtype=jnp.int32) == my_seq).astype(jnp.float32)
    seq_sums = lax.psum(seq_onehot * own_sum, ("ctx", "head"))
    margins = seq_sums[0::2] - seq_sums[1::2]
    pair_coef = jax.nn.sigmoid(hinge_sharp * (hinge_margin - margins))
    seq_grad = jnp.stack([-pair_coef, pair_coef], axis=1).reshape(seq_count)
    my_grad = jnp.sum(seq_onehot * seq_grad)
    cotangent = (mask_float * my_grad)[:, None, None, None] * directions
    grad_state = reverse_carry(
        (
            block_decay * keep_reverse,
            jnp.einsum(
                "tghp,tgn->ghpn", cotangent * growth, c_float, precision=lax.Precision.HIGHEST
            )
            * keep_reverse,
        )
    )
    grad_x_out, grad_step_out, grad_cum, grad_skip_local, grad_b_out, grad_c, unused = pull_output(
        cotangent
    )
    grad_decay = jnp.sum(grad_state * state_in, axis=(2, 3))
    grad_x_state, grad_step_state, grad_rate_local, grad_b_state = pull_state(
        (grad_state, grad_decay, grad_cum)
    )
    grad_x = grad_x_state + grad_x_out
    grad_step = grad_step_state + grad_step_out
    grad_b = grad_b_state + grad_b_out
    grad_cols = jnp.stack([grad_b, grad_c], axis=2).reshape(tok_count, column_count)
    columns = hidden
    grad_w = lax.psum_scatter(
        lax.dot_general(
            columns, grad_cols, (((0,), (0,)), ((), ())), preferred_element_type=jnp.float32
        ),
        "ctx",
        scatter_dimension=0,
        tiled=True,
    )
    rate_total, skip_total = lax.psum(
        (grad_rate_local.reshape(head_count), grad_skip_local.reshape(head_count)), "ctx"
    )
    return (
        grad_x.reshape(tok_count, head_count * HEADDIM),
        grad_step.reshape(head_count, tok_count),
        rate_total,
        skip_total,
        grad_w,
    )


def solution(mesh):
    return jax.shard_map(
        body,
        mesh=mesh,
        in_specs=(
            P("ctx", None),
            P("ctx", "head"),
            P("ctx", "head"),
            P("head", "ctx"),
            P("head"),
            P("head"),
            P("ctx", "head"),
            P("ctx"),
            P(),
            P("ctx"),
        ),
        out_specs=(P("ctx", "head"), P("head", "ctx"), P("head"), P("head"), P("ctx", "head")),
        check_vma=False,
    )
```

profile of v0, /device:TPU:1, one launch (start us, length us, event | category | flops | bytes accessed | tf_op | source)
XLA Modules:
  0.0 761.5 jit_solution(15901357721924093078)
XLA Ops:
  14.9 1.4 fusion.57
  16.3 84.4 %all-gather.8.cloned.1.call-done = bf16[4096,256]{1,0:T(8,128)(2,1)} async-done(((bf16[64,256]{1,0:T(8,128)(2,1)}), bf16[4096,256]{1,0:T(8,128)(2,1)}) %all-gather.8.cloned.1.call-update) | async-done | bytes 2097168 | tf_op jit(solution)/shard_map/all_gather | solution.py:102
  100.7 2.5 convolution_convert_fusion.4
  106.2 38.0 %all-gather.1 = f32[64,8,1]{1,2,0:T(1,128)S(1)} all-gather(f32[1,8,1]{1,2,0:T(1,128)S(1)} %copy.91), channel_id=3, replica_groups=mesh['ctx'=64,'head'=8] {'ctx'}, dimensions={0}, use_global_device_ids=true | all-gather | bytes 2080 | tf_op jit(solution)/shard_map/all_gather | solution.py:16
  145.8 62.0 %all-gather.10.cloned.1.call-done = f32[512,64,128]{2,1,0:T(8,128)} async-done(((f32[8,64,128]{2,1,0:T(8,128)}), f32[512,64,128]{2,1,0:T(8,128)}) %all-gather.10.cloned.1.call-update) | async-done | bytes 16777232 | tf_op jit(solution)/shard_map/all_gather | solution.py:16
  207.8 70.1 %while.30 = (s32[]{:T(128)}, f32[1,8,64,128]{3,2,1,0:T(8,128)S(1)}, s32[]{:T(128)}, f32[64,1,8]{2,1,0:T(1,128)S(1)}, f32[64,1,8,64,128]{4,3,2,1,0:T(8,128)}, /*index=5*/s32[]{:T(128)}, s32[]{:T(128)}) while((s32[]{:T(128)}, f32[1,8,64,128]{3,2,1,0:T(8,128)S(1)}, s32[]{:T(128)}, f32[64,1,8]{2,1,0:T(1,128)S(1)}, ...), condition=%wide.region_7.8_spmd.clone, body=%wide.region_6.7_spmd.clone.sunk | while | flops 262148 | bytes 786641 | solution.py:27
  278.3 1.8 fusion.12
  282.6 95.4 %psum.21 = f32[4]{0:T(128)} all-reduce(f32[4]{0:T(128)} %compare_select_fusion), channel_id=1, replica_groups=mesh['ctx'=64,'head'=8] {'ctx','head'}, use_global_device_ids=true, to_apply=%region_11.12 | all-reduce | flops 4 | bytes 32 | tf_op jit(solution)/shard_map/psum | solution.py:131
  381.8 1.3 convert_multiply_fusion
  386.3 43.1 %all-gather = f32[64,8,1]{1,2,0:T(1,128)} all-gather(f32[1,8,1]{1,2,0:T(1,128)} %copy.86), channel_id=2, replica_groups=mesh['ctx'=64,'head'=8] {'ctx'}, dimensions={0}, use_global_device_ids=true | all-gather | bytes 2080 | tf_op jit(solution)/shard_map/all_gather | solution.py:16
  429.5 3.5 fusion.5
  435.1 53.3 %all-gather.12.cloned.1.call-done = f32[512,64,128]{2,1,0:T(8,128)} async-done(((f32[8,64,128]{2,1,0:T(8,128)}), f32[512,64,128]{2,1,0:T(8,128)}) %all-gather.12.cloned.1.call-update) | async-done | bytes 16777232 | tf_op jit(solution)/shard_map/all_gather | solution.py:16
  488.4 110.2 %while.31 = (s32[]{:T(128)}, f32[1,8,64,128]{3,2,1,0:T(8,128)S(1)}, s32[]{:T(128)}, f32[64,1,8]{2,1,0:T(1,128)}, f32[64,1,8,64,128]{4,3,2,1,0:T(8,128)}, /*index=5*/s32[]{:T(128)}, s32[]{:T(128)}, s32[]{:T(128)}, s32[]{:T(128)}) while((s32[]{:T(128)}, f32[1,8,64,128]{3,2,1,0:T(8,128)S(1)}, s32[]{:T(128)}, ...), condition=%wide.region_14.15_spmd.clone, body=%wide.region_13.14_spmd.clone.sunk | while | flops 262152 | bytes 786703 | solution.py:27
  598.7 1.9 multiply_reduce_fusion.2
  602.5 2.7 convolution_bitcast_fusion
  605.2 5.6 copy.107
  610.9 1.4 reduce_sum.204
  612.3 1.3 reduce_sum.205
  613.6 1.3 multiply_reduce_fusion.5
  617.0 2.5 reduce-window.32
  619.6 1.5 multiply_reduce_fusion.7
  621.2 124.5 %all-reduce.1 = (f32[8]{0:T(128)}, f32[8]{0:T(128)}) all-reduce(f32[8]{0:T(128)S(1)} %get-tuple-element.386, f32[8]{0:T(128)} %reduce_sum.205), channel_id=1, replica_groups=mesh['ctx'=64,'head'=8] {'ctx'}, use_global_device_ids=true, to_apply=%region_25.26 | all-reduce | flops 16 | bytes 128 | tf_op jit(solution)/shard_map/psum | solution.py:166
  746.9 1.7 fusion.17
  749.5 5.5 reduce-scatter.4.cloned.1.call-done
  (345 shorter events, 203.2 us)
Async XLA Ops:
  7.2 93.6 %copy-start = (bf16[256,4096]{1,0:T(8,128)(2,1)S(1)}, bf16[256,4096]{1,0:T(8,128)(2,1)}, u32[]{:S(2)}) copy-start(bf16[256,4096]{1,0:T(8,128)(2,1)} %param.14) | copy-start | bytes 6291460
  7.2 93.5 %all-gather.8.cloned.1.call-start = ((), (), s32[]{:S(2)}) async-start(), calls=%async_computation.1 | async-start | bytes 2129920 | tf_op jit(solution)/shard_map/all_gather | solution.py:102
  7.9 199.9 %all-gather.10.cloned.1.call-start = ((), (), s32[]{:S(2)}) async-start(), calls=%async_computation.2 | async-start | bytes 17039360 | tf_op jit(solution)/shard_map/all_gather | solution.py:16
  14.0 369.1 %copy-start.1 = (bf16[256,512]{0,1:T(8,128)(2,1)}, bf16[256,512]{0,1:T(8,128)(2,1)S(1)}, u32[]{:S(2)}) copy-start(bf16[256,512]{0,1:T(8,128)(2,1)S(1)} %copy.90) | copy-start | bytes 786436
  14.1 89.1 %copy-start.8 = (f32[1,8,256]{2,1,0:T(8,128)}, f32[1,8,256]{2,1,0:T(8,128)S(1)}, u32[]{:S(2)}) copy-start(f32[1,8,256]{2,1,0:T(8,128)S(1)} %get-tuple-element.381) | copy-start | bytes 24580
  14.9 88.4 %copy-start.14 = (f32[8]{0:T(128)}, f32[8]{0:T(128)S(1)}, u32[]{:S(2)}) copy-start(f32[8]{0:T(128)S(1)} %get-tuple-element.389) | copy-start | bytes 100
  16.3 87.1 %copy-start.10 = (f32[8,256]{1,0:T(8,128)}, f32[8,256]{1,0:T(8,128)S(1)}, u32[]{:S(2)}) copy-start(f32[8,256]{1,0:T(8,128)S(1)} %get-tuple-element.382) | copy-start | bytes 24580
  16.3 88.5 %copy-start.6 = (bf16[256,512]{1,0:T(8,128)(2,1)S(1)}, bf16[256,512]{1,0:T(8,128)(2,1)}, u32[]{:S(2)}) copy-start(bf16[256,512]{1,0:T(8,128)(2,1)} %param.20) | copy-start | bytes 786436
  16.3 88.7 %copy-start.16 = (s32[4]{0:T(128)S(1)}, s32[4]{0:T(128)}, u32[]{:S(2)}) copy-start(s32[4]{0:T(128)} %param.22) | copy-start | bytes 52
  103.3 1.4 copy-start.2
  103.4 1.3 copy-start.4
  104.6 383.8 %all-gather.12.cloned.1.call-start = ((), (), s32[]{:S(2)}) async-start(), calls=%async_computation.3 | async-start | bytes 17039360 | tf_op jit(solution)/shard_map/all_gather | solution.py:16
  207.8 70.5 %copy-start.7 = (f32[8,256]{1,0:T(8,128)S(1)}, f32[8,256]{1,0:T(8,128)}, u32[]{:S(2)}) copy-start(f32[8,256]{1,0:T(8,128)} %param.17) | copy-start | bytes 24580
  278.3 1.9 copy-start.15
  278.3 1.8 copy-start.17
  383.1 0.8 copy-start.12
  385.0 370.0 %reduce-scatter.4.cloned.1.call-start = ((), (), s32[]{:S(2)}) async-start(), calls=%async_computation.4 | async-start | bytes 4259840
  429.5 4.4 copy-start.13
  433.0 0.7 copy-start.3
  488.4 110.2 %copy-start.11 = (f32[8,256]{1,0:T(8,128)S(1)}, f32[8,256]{1,0:T(8,128)}, u32[]{:S(2)}) copy-start(f32[8,256]{1,0:T(8,128)} %copy-done.10) | copy-start | bytes 24580
  610.8 5.3 copy-start.9
  610.8 134.9 %copy-start.5 = (f32[256,128]{1,0:T(8,128)S(1)}, f32[256,128]{1,0:T(8,128)}, u32[]{:S(2)}) copy-start(f32[256,128]{1,0:T(8,128)} %copy-done.4) | copy-start | bytes 393220
Sparse Core Ops, SparseCore 0:
  11.4 89.2 all-gather.7
  104.8 103.0 all-gather.9
  385.1 103.2 all-gather.11
  611.0 143.9 reduce-scatter.3
where the time goes:
time: 771 us; the launch traced here: 762 us
  blocking collectives  301 us (39%)
  waiting for transfers between devices  206 us (27%)
  other arithmetic  156 us (20%)
  local copies, waits for them, and re-layouts  55.6 us (7%)
  matrix products  21.5 us (3%)
  between operations  17.3 us (2%)
    select_n x128, other arithmetic, hop(): return jax.tree.map(lambda a, b: jnp.where(reached, a, b), new, before)  135 us
    psum x1, blocking collectives, body(): lax.psum((grad_rate_local.reshape(head_count), grad_skip_local.reshape(he...  124 us
    all_gather x2, waiting for transfers between devices, prefix(): everything = jax.tree.map(lambda part: lax.all_gather(part, axis), x)  115 us
    psum x1, blocking collectives, body(): seq_sums = lax.psum(seq_onehot * own_sum, ('ctx', 'head'))  95.4 us
    all_gather x1, waiting for transfers between devices, body(): lax.all_gather(w_bc, 'ctx', axis=0, tiled=True)  84.4 us
    all_gather x2, blocking collectives, prefix(): everything = jax.tree.map(lambda part: lax.all_gather(part, axis), x)  81.1 us
    mul x128, local copies, waits for them, and re-layouts, chain_pair(): later_part[0][:, :, None, None] * earlier[1] + later_part[1]  41.5 us
  transfers between devices with their start and end apart: 4, of which 4 were waited for; matrix products, arithmetic and copies ran while one was open for 4% of the time, Pallas kernels for 0%

commit v1 on v0

v1 whole, which is shorter than its diff:
```python
import functools

import jax
import jax.numpy as jnp
from jax import lax
from jax.experimental import pallas as pl
from jax.experimental.pallas import tpu as pltpu
from jax.sharding import PartitionSpec as P

HEADDIM = 64
NSTATE = 128
NX, NZ, NC = 4, 8, 2
NCTX = NX * NZ * NC
NHEAD = 8
TOK = 256
HEADS = 8
WIDE = HEADS * HEADDIM
DEPTH = 64
COLS = 2 * NSTATE
MODEL = NCTX * DEPTH
PART = 48

hinge_sharp = 0.005
hinge_margin = 10.0

MESH = pl.DeviceIdType.MESH
F32 = jnp.float32
BF16 = jnp.bfloat16
VMEM_LIMIT = 48 << 20


def place():
    index = lax.axis_index("ctx")
    return index // 16, (index // 2) % 8, index % 2, lax.axis_index("head")


def at(x, z, c, head):
    return (((x % NX) * NZ + (z % NZ)) * NC + c, head)


def greet(partners):
    barrier = pltpu.get_barrier_semaphore()
    for partner in partners:
        pl.semaphore_signal(barrier, inc=1, device_id=partner, device_id_type=MESH)
    pl.semaphore_wait(barrier, len(partners))


def plane_partners(x, z, c, head):
    return (
        [at(x, z + dz, c, head) for dz in range(1, NZ)]
        + [at(x + dx, z, c, head) for dx in range(1, NX)]
        + [at(x, z, 1 - c, head)]
    )


def dot(left, right, dims=((1,), (0,)), precision=None):
    return lax.dot_general(left, right, (dims, ((), ())), precision=precision, preferred_element_type=F32)


def gather_kernel(w_ref, step_ref, rate_ref, hid_ref, bc_ref, dec_ref, buf, hid, load_sem, ss, rs):
    x, z, c, head = place()
    load = pltpu.make_async_copy(hid_ref, hid, load_sem)
    load.start()
    greet(plane_partners(x, z, c, head))
    buf[x, z, c] = w_ref[...]
    rows = lax.broadcasted_iota(jnp.int32, (8, 128), 0)
    lanes = lax.broadcasted_iota(jnp.int32, (8, 128), 1)
    total = jnp.sum(step_ref[...], axis=1, keepdims=True)
    spread = jnp.zeros((8, 128), F32)
    for h in range(HEADS):
        spread = jnp.where((rows == h) & (lanes == h), -rate_ref[h] * total, spread)
    dec_ref[x, z, c] = jnp.sum(spread, axis=0, keepdims=True)

    started = []

    def send(ref, index, k, partner):
        piece = ref.at[index]
        copy = pltpu.make_async_remote_copy(
            piece, piece, ss.at[k], rs.at[k], device_id=partner, device_id_type=MESH
        )
        copy.start()
        started.append(copy)

    def arrive(ref, index, k):
        piece = ref.at[index]
        pltpu.make_async_remote_copy(
            piece, piece, ss.at[k], rs.at[k], device_id=at(x, z, 1 - c, head), device_id_type=MESH
        ).wait_recv()

    every = slice(None)
    low, high = pl.ds(0, PART), pl.ds(PART, DEPTH - PART)
    for dz in (4, 3, 5, 2, 6, 1, 7):
        send(buf, (x, z, c, low), dz - 1, at(x, z + dz, c, head))
        send(dec_ref, (x, z, c), 24 + dz, at(x, z + dz, c, head))
    for dx in (2, 1, 3):
        send(buf, (x, z, c, high), 6 + dx, at(x + dx, z, c, head))
    for dz in range(1, NZ):
        arrive(buf, (x, (z - dz) % NZ, c, low), dz - 1)
    for dx in (2, 1, 3):
        send(buf, (x, every, c, low), 9 + dx, at(x + dx, z, c, head))
    for dx in range(1, NX):
        arrive(buf, ((x - dx) % NX, z, c, high), 6 + dx)
    for dz in (4, 3, 5, 2, 6, 1, 7):
        send(buf, (every, z, c, high), 12 + dz, at(x, z + dz, c, head))
    send(buf, (x, every, c, low), 20, at(x, z, 1 - c, head))
    for dz in range(1, NZ):
        arrive(dec_ref, (x, (z - dz) % NZ, c), 24 + dz)
    for dx in range(1, NX):
        send(dec_ref, (x, every, c), 31 + dx, at(x + dx, z, c, head))
    for dz in range(1, NZ):
        arrive(buf, (every, (z - dz) % NZ, c, high), 12 + dz)
    send(buf, (every, every, c, high), 24, at(x, z, 1 - c, head))
    for dx in (1, 3, 2):
        arrive(buf, ((x - dx) % NX, every, c, low), 9 + dx)
        send(buf, ((x - dx) % NX, every, c, low), 20 + dx, at(x, z, 1 - c, head))
    for dx in range(1, NX):
        arrive(dec_ref, ((x - dx) % NX, every, c), 31 + dx)
    send(dec_ref, (every, every, c), 35, at(x, z, 1 - c, head))
    load.wait()
    arrive(buf, (every, every, 1 - c, high), 24)
    arrive(buf, (x, every, 1 - c, low), 20)
    for dx in (1, 3, 2):
        arrive(buf, ((x - dx) % NX, every, 1 - c, low), 20 + dx)
    span = MODEL // NX
    sums = jnp.zeros((TOK, COLS), F32)
    for part in range(NX):
        sums = sums + dot(hid[:, part * span : (part + 1) * span], buf[part].reshape(span, COLS))
    bc_ref[...] = sums.astype(BF16)
    arrive(dec_ref, (every, every, 1 - c), 35)
    for copy in started:
        copy.wait_send()


def gather(w_bc, step_size, decay_rate, hidden):
    vmem = pl.BlockSpec(memory_space=pltpu.VMEM)
    return pl.pallas_call(
        gather_kernel,
        name="gather_project",
        out_shape=(
            jax.ShapeDtypeStruct((TOK, COLS), BF16),
            jax.ShapeDtypeStruct((NX, NZ, NC, 1, 128), F32),
        ),
        in_specs=[
            vmem,
            vmem,
            pl.BlockSpec(memory_space=pltpu.SMEM),
            pl.BlockSpec(memory_space=pl.ANY),
        ],
        out_specs=(vmem, vmem),
        scratch_shapes=[
            pltpu.VMEM((NX, NZ, NC, DEPTH, COLS), BF16),
            pltpu.VMEM((TOK, MODEL), BF16),
            pltpu.SemaphoreType.DMA,
            pltpu.SemaphoreType.DMA((36,)),
            pltpu.SemaphoreType.DMA((36,)),
        ],
        compiler_params=pltpu.CompilerParams(
            collective_id=0, has_side_effects=True, vmem_limit_bytes=VMEM_LIMIT
        ),
    )(w_bc, step_size, decay_rate, hidden)


def pair_columns(columns, base, pair, low_half):
    one, two = base + 2 * pair, base + 2 * pair + 1
    return jnp.where(low_half, columns[:, one : one + 1], columns[:, two : two + 1])


def sequence_starts(stretch_ref):
    one = stretch_ref[0]
    two = one + stretch_ref[1]
    return one, two, two + stretch_ref[2]


def local_kernel(
    bc_ref, x_ref, dir_ref, step_ref, mask_ref, base_ref, dec_ref, rate_ref, skip_ref, stretch_ref,
    msg_ref, tab_ref, own_ref, gbc_ref, gx_ref, rows_ref, cols_ref, xf_ref, dyg_ref, small_ref,
    stack, drow,
):
    index, head = lax.axis_index("ctx"), lax.axis_index("head")
    step = step_ref[...]
    row8 = lax.broadcasted_iota(jnp.int32, (8, TOK), 0)
    rate = jnp.zeros((8, TOK), F32)
    for h in range(HEADS):
        rate = jnp.where(row8 == h, rate_ref[h], rate)
    s_index = lax.broadcasted_iota(jnp.int32, (TOK, TOK), 0)
    t_index = lax.broadcasted_iota(jnp.int32, (TOK, TOK), 1)
    causal = s_index <= t_index
    cum = -rate * dot(step, causal.astype(F32), precision=lax.Precision.HIGHEST)
    last = cum[:, TOK - 1 : TOK]
    mask = mask_ref[...].astype(F32)
    stack[...] = jnp.zeros((128, TOK), F32)
    stack[0:8] = cum - jnp.log(step)
    stack[8:16] = jnp.exp(cum)
    stack[16:24] = jnp.exp(last - cum) * step
    stack[24:32] = jnp.broadcast_to(mask, (8, TOK))
    columns = stack[...].T
    cols_ref[...] = columns
    rows_ref[0:8] = cum

    bc = bc_ref[...]
    b_in, c_in = bc[:, :NSTATE], bc[:, NSTATE:]
    low_half = lax.broadcasted_iota(jnp.int32, (TOK, 128), 1) < HEADDIM
    mask_column = columns[:, 24:25]
    scores = dot(b_in, c_in, ((1,), (1,)))
    grad_scores = jnp.zeros((TOK, TOK), F32)
    back = jnp.zeros((TOK, 128), F32)
    lane128 = lax.broadcasted_iota(jnp.int32, (TOK, 128), 1)
    overlap = []
    for pair in range(HEADS // 2):
        span = slice(128 * pair, 128 * pair + 128)
        x_pair = x_ref[:, span]
        x_wide = x_pair.astype(F32)
        dy_wide = dir_ref[:, span].astype(F32) * mask_column
        dy_pair = dy_wide.astype(BF16)
        xf_ref[:, span] = (x_wide * pair_columns(columns, 16, pair, low_half)).astype(BF16)
        dyg_ref[:, span] = (dy_wide * pair_columns(columns, 8, pair, low_half)).astype(BF16)
        overlap.append(jnp.sum(x_wide * dy_wide, axis=0, keepdims=True))
        within = []
        for h in (2 * pair, 2 * pair + 1):
            half = slice(HEADDIM * (h % 2), HEADDIM * (h % 2) + HEADDIM)
            x_h, dy_h = x_pair[:, half], dy_pair[:, half]
            gap = jnp.where(causal, cum[h : h + 1, :] - columns[:, h : h + 1], -1e30)
            factor = jnp.exp(gap)
            moved = dot(x_h, dy_h, ((1,), (1,))) * factor
            grad_scores = grad_scores + moved
            spent = moved * scores
            drow[h : h + 1] = jnp.sum(spent, axis=0, keepdims=True)
            back = jnp.where(lane128 == h, jnp.sum(spent, axis=1, keepdims=True), back)
            within.append(dot((scores * factor).astype(BF16), dy_h))
        skip_pair = jnp.where(low_half, skip_ref[2 * pair], skip_ref[2 * pair + 1])
        gx_ref[:, span] = jnp.concatenate(within, axis=1) + skip_pair * dy_wide
    rows_ref[8:16] = drow[...]
    rows_ref[16:24] = back.T[0:8]
    local = dot(xf_ref[...], b_in, ((0,), (0,)))
    grown = dot(dyg_ref[...], c_in, ((0,), (0,)))
    msg_ref[...] = jnp.concatenate(
        [local.reshape(NCTX, 8, 128), grown.reshape(NCTX, 8, 128)], axis=1
    ).astype(BF16)
    grad_bf = grad_scores.astype(BF16)
    gbc_ref[:, :NSTATE] = dot(grad_bf, c_in)
    gbc_ref[:, NSTATE:] = dot(grad_bf, b_in, ((0,), (0,)))

    wide_row = lax.broadcasted_iota(jnp.int32, (WIDE, 128), 0) // HEADDIM
    wide_lane = lax.broadcasted_iota(jnp.int32, (WIDE, 128), 1)
    picks = (wide_row == wide_lane).astype(F32)
    overlap_row = jnp.broadcast_to(jnp.concatenate(overlap, axis=1), (8, WIDE))
    overlap_head = dot(overlap_row, picks, precision=lax.Precision.HIGHEST)
    small_ref[...] = overlap_head
    lane8 = lax.broadcasted_iota(jnp.int32, (8, 128), 1)
    skip_row = jnp.zeros((8, 128), F32)
    for h in range(HEADS):
        skip_row = jnp.where(lane8 == h, skip_ref[h], skip_row)
    pieces = jnp.sum(grad_scores * scores, axis=0, keepdims=True)
    pieces = pieces + jnp.where(head == 0, 1.0, 0.0) * mask * base_ref[...]
    own = pieces[:, :128] + pieces[:, 128:] + (overlap_head * skip_row)[0:1]

    one, two, three = sequence_starts(stretch_ref)
    my_seq = (
        (index >= one).astype(jnp.int32)
        + (index >= two).astype(jnp.int32)
        + (index >= three).astype(jnp.int32)
    )
    own_ref[...] = jnp.where(lax.broadcasted_iota(jnp.int32, (8, 128), 0) == my_seq, own, 0.0)
    block = lax.broadcasted_iota(jnp.int32, (NCTX, 128), 0)
    lane64 = lax.broadcasted_iota(jnp.int32, (NCTX, 128), 1)
    decs = jnp.concatenate(
        [dec_ref[b // 16, (b // 2) % 8, b % 2] for b in range(NCTX)], axis=0
    )
    mine = jnp.sum(jnp.where(lane64 == index // 8, decs, 0.0), axis=1, keepdims=True)
    tab_ref[0] = jnp.broadcast_to(jnp.exp(mine), (NCTX, 128))
    begins = (block == 0) | (block == one) | (block == two) | (block == three)
    tab_ref[1] = jnp.where(begins, 0.0, 1.0)
    final = (block == NCTX - 1) | (block == one - 1) | (block == two - 1) | (block == three - 1)
    tab_ref[2] = jnp.where(final, 0.0, 1.0)
    seq = (
        (block >= one).astype(jnp.int32)
        + (block >= two).astype(jnp.int32)
        + (block >= three).astype(jnp.int32)
    )
    for j in range(4):
        tab_ref[3 + j] = jnp.where(seq == j, 1.0, 0.0)


def local_part(bc, x_act, logp_dir, step_size, mask, base, dec, rate, skip, stretches):
    vmem = pl.BlockSpec(memory_space=pltpu.VMEM)
    smem = pl.BlockSpec(memory_space=pltpu.SMEM)
    shape = jax.ShapeDtypeStruct
    return pl.pallas_call(
        local_kernel,
        name="local_part",
        out_shape=(
            shape((NCTX, 16, 128), BF16),
            shape((7, NCTX, 128), F32),
            shape((8, 128), F32),
            shape((TOK, COLS), F32),
            shape((TOK, WIDE), F32),
            shape((24, TOK), F32),
            shape((TOK, 128), F32),
            shape((TOK, WIDE), BF16),
            shape((TOK, WIDE), BF16),
            shape((8, 128), F32),
        ),
        in_specs=[vmem] * 7 + [smem] * 3,
        out_specs=tuple([vmem] * 10),
        scratch_shapes=[pltpu.VMEM((128, TOK), F32), pltpu.VMEM((8, TOK), F32)],
        compiler_params=pltpu.CompilerParams(vmem_limit_bytes=VMEM_LIMIT),
    )(bc, x_act, logp_dir, step_size, mask, base, dec, rate, skip, stretches)


def scan_kernel(
    msg_ref, tab_ref, own_ref, out_ref, sums_ref,
    got, wide, swept, reply, part, near, far, across, send_sem, recv_sem, ss, rs,
):
    index = lax.axis_index("ctx")
    x, z, c, head = place()
    barrier = pltpu.get_barrier_semaphore()

    def hello(k, carry):
        pl.semaphore_signal(
            barrier, inc=1, device_id=((index + k) % NCTX, head), device_id_type=MESH
        )
        return carry

    def hello_head(k, carry):
        pl.semaphore_signal(
            barrier, inc=1, device_id=(index, (head + k) % NHEAD), device_id_type=MESH
        )
        return carry

    lax.fori_loop(1, NCTX, hello, 0)
    lax.fori_loop(1, NHEAD, hello_head, 0)
    pl.semaphore_wait(barrier, NCTX - 1 + NHEAD - 1)

    def exchange(source, target, phase):
        def start(k, carry):
            to = (index + k) % NCTX
            pltpu.make_async_remote_copy(
                source.at[to],
                target.at[index],
                send_sem.at[phase],
                recv_sem.at[phase],
                device_id=(to, head),
                device_id_type=MESH,
            ).start()
            return carry

        lax.fori_loop(1, NCTX, start, 0)

    def settle(target, sem):
        rest = target.at[pl.ds(0, NCTX - 1)]
        pltpu.make_async_copy(rest, rest, sem).wait()

    exchange(msg_ref, got, 0)
    got[index] = msg_ref[index]
    settle(got, recv_sem.at[0])
    wide[...] = got[...].astype(F32)

    def step(b, carry):
        state, grad = carry
        r = NCTX - 1 - b
        state = state * tab_ref[1, pl.ds(b, 1)]
        grad = grad * tab_ref[2, pl.ds(r, 1)]
        swept[b, 0:8] = state
        swept[r, 8:16] = grad
        state = state * tab_ref[0, pl.ds(b, 1)] + wide[b, 0:8]
        grad = grad * tab_ref[0, pl.ds(r, 1)] + wide[r, 8:16]
        return state, grad

    zero = jnp.zeros((8, 128), F32)
    lax.fori_loop(0, NCTX, step, (zero, zero))
    reply[...] = swept[...].astype(BF16)
    exchange(reply, out_ref, 1)
    out_ref[index] = reply[index]

    met = jnp.sum(swept[:, 0:8] * wide[:, 8:16], axis=1)
    row = lax.broadcasted_iota(jnp.int32, (8, 128), 0)
    total = own_ref[...]
    for j in range(4):
        total = total + jnp.where(
            row == j, jnp.sum(met * tab_ref[3 + j], axis=0, keepdims=True), 0.0
        )
    part[0] = total

    started = []

    def share(source, target, k, partner):
        copy = pltpu.make_async_remote_copy(
            source, target, ss.at[k], rs.at[k], device_id=partner, device_id_type=MESH
        )
        copy.start()
        started.append(copy)
        return copy

    copies = []
    for k in range(1, 16):
        to = (index // 16) * 16 + (index + k) % 16
        copies.append(share(part.at[0], near.at[k - 1], k - 1, (to, head)))
    for copy in copies:
        copy.wait_recv()
    part[1] = part[0] + jnp.sum(near[...], axis=0)
    copies = []
    for k in range(1, NX):
        copies.append(share(part.at[1], far.at[k - 1], 14 + k, at(x + k, z, c, head)))
    for copy in copies:
        copy.wait_recv()
    part[2] = part[1] + jnp.sum(far[...], axis=0)
    copies = []
    for k in range(1, NHEAD):
        copies.append(share(part.at[2], across.at[k - 1], 17 + k, (index, (head + k) % NHEAD)))
    for copy in copies:
        copy.wait_recv()
    sums_ref[...] = part[2] + jnp.sum(across[...], axis=0)
    for copy in started:
        copy.wait_send()
    settle(msg_ref, send_sem.at[0])
    settle(reply, send_sem.at[1])
    settle(out_ref, recv_sem.at[1])


def scan_part(msg, tab, own):
    vmem = pl.BlockSpec(memory_space=pltpu.VMEM)
    shape = jax.ShapeDtypeStruct
    return pl.pallas_call(
        scan_kernel,
        name="scan_part",
        out_shape=(shape((NCTX, 16, 128), BF16), shape((8, 128), F32)),
        in_specs=[vmem] * 3,
        out_specs=(vmem, vmem),
        scratch_shapes=[
            pltpu.VMEM((NCTX, 16, 128), BF16),
            pltpu.VMEM((NCTX, 16, 128), F32),
            pltpu.VMEM((NCTX, 16, 128), F32),
            pltpu.VMEM((NCTX, 16, 128), BF16),
            pltpu.VMEM((3, 8, 128), F32),
            pltpu.VMEM((15, 8, 128), F32),
            pltpu.VMEM((NX - 1, 8, 128), F32),
            pltpu.VMEM((NHEAD - 1, 8, 128), F32),
            pltpu.SemaphoreType.DMA((2,)),
            pltpu.SemaphoreType.DMA((2,)),
            pltpu.SemaphoreType.DMA((25,)),
            pltpu.SemaphoreType.DMA((25,)),
        ],
        compiler_params=pltpu.CompilerParams(
            collective_id=1, has_side_effects=True, vmem_limit_bytes=VMEM_LIMIT
        ),
    )(msg, tab, own)


def halves(value):
    top = value.astype(BF16)
    return top, (value - top.astype(F32)).astype(BF16)


def grad_kernel(
    states_ref, sums_ref, bc_ref, x_ref, xf_ref, dyg_ref, gbc_ref, gx_ref, rows_ref, cols_ref, small_ref,
    step_ref, rate_ref, stretch_ref,
    grad_x_ref, grad_step_ref, grad_cols_ref, few_ref,
):
    index = lax.axis_index("ctx")
    one, two, three = sequence_starts(stretch_ref)
    seq_sums = jnp.sum(sums_ref[...], axis=1, keepdims=True)
    first = seq_sums[0:1] - seq_sums[1:2]
    second = seq_sums[2:3] - seq_sums[3:4]
    margin = jnp.where(index >= two, second, first)
    coef = 1.0 / (1.0 + jnp.exp(-hinge_sharp * (hinge_margin - margin)))
    rejected = ((index >= one) & (index < two)) | (index >= three)
    scale = jnp.where(rejected, coef, -coef)

    states = states_ref[...].astype(F32)
    state_in = states[:, 0:8].reshape(WIDE, NSTATE)
    grad_state = states[:, 8:16].reshape(WIDE, NSTATE)
    state_bf, grad_bf = state_in.astype(BF16), grad_state.astype(BF16)
    bc = bc_ref[...]
    b_in, c_in = bc[:, :NSTATE], bc[:, NSTATE:]
    columns = cols_ref[...]
    low_half = lax.broadcasted_iota(jnp.int32, (TOK, 128), 1) < HEADDIM
    pick_row = lax.broadcasted_iota(jnp.int32, (8, 128), 0)
    pick_half = lax.broadcasted_iota(jnp.int32, (8, 128), 1) // HEADDIM
    nt = ((1,), (1,))
    carried = jnp.zeros((8, TOK), F32)
    kept = jnp.zeros((8, TOK), F32)
    for pair in range(HEADS // 2):
        span = slice(128 * pair, 128 * pair + 128)
        picks = (pick_row == 2 * pair + pick_half).astype(BF16)
        left = dot(c_in, state_bf[span], nt) * dyg_ref[:, span].astype(F32)
        top, low = halves(left)
        carried = carried + dot(picks, top, nt) + dot(picks, low, nt)
        back = dot(b_in, grad_bf[span], nt) * pair_columns(columns, 16, pair, low_half)
        top, low = halves(back * x_ref[:, span].astype(F32))
        kept = kept + dot(picks, top, nt) + dot(picks, low, nt)
        grad_x_ref[:, span] = ((gx_ref[:, span] + back) * scale).astype(BF16)
    grad_b = gbc_ref[:, :NSTATE] + dot(xf_ref[...], grad_bf)
    grad_c = gbc_ref[:, NSTATE:] + dot(dyg_ref[...], state_bf)
    grad_cols_ref[:, :NSTATE] = (grad_b * scale).astype(BF16)
    grad_cols_ref[:, NSTATE:] = (grad_c * scale).astype(BF16)

    cum, drow, dcol = rows_ref[0:8], rows_ref[8:16], rows_ref[16:24]
    step = step_ref[...]
    row8 = lax.broadcasted_iota(jnp.int32, (8, TOK), 0)
    rate = jnp.zeros((8, TOK), F32)
    for h in range(HEADS):
        rate = jnp.where(row8 == h, rate_ref[h], rate)
    grad_decay = jnp.sum(
        jnp.sum((state_in * grad_state).reshape(HEADS, HEADDIM, NSTATE), axis=1), axis=1, keepdims=True
    )
    end = jnp.sum(kept, axis=1, keepdims=True) + grad_decay * jnp.exp(cum[:, TOK - 1 : TOK])
    token = lax.broadcasted_iota(jnp.int32, (8, TOK), 1)
    grad_cum = drow - dcol + carried - kept + jnp.where(token == TOK - 1, end, 0.0)
    t_index = lax.broadcasted_iota(jnp.int32, (TOK, TOK), 0)
    u_index = lax.broadcasted_iota(jnp.int32, (TOK, TOK), 1)
    tail = dot(grad_cum, (t_index >= u_index).astype(F32), precision=lax.Precision.HIGHEST)
    grad_step_ref[...] = ((dcol + kept) / step - rate * tail) * scale
    grad_rate = -jnp.sum(step * tail, axis=1, keepdims=True)
    lane = lax.broadcasted_iota(jnp.int32, (8, 128), 1)
    rate_row = jnp.sum(jnp.where(lane == pick_row, grad_rate, 0.0), axis=0, keepdims=True)
    few_ref[...] = jnp.where(pick_row == 0, rate_row, small_ref[...]) * scale


def grad_part(states, sums, bc, x_act, xf, dyg, gbc, gx, rows, cols, small, step_size, rate, stretches):
    vmem = pl.BlockSpec(memory_space=pltpu.VMEM)
    smem = pl.BlockSpec(memory_space=pltpu.SMEM)
    shape = jax.ShapeDtypeStruct
    return pl.pallas_call(
        grad_kernel,
        name="grad_part",
        out_shape=(
            shape((TOK, WIDE), BF16),
            shape((8, TOK), F32),
            shape((TOK, COLS), BF16),
            shape((8, 128), F32),
        ),
        in_specs=[vmem] * 12 + [smem] * 2,
        out_specs=tuple([vmem] * 4),
        compiler_params=pltpu.CompilerParams(vmem_limit_bytes=VMEM_LIMIT),
    )(states, sums, bc, x_act, xf, dyg, gbc, gx, rows, cols, small, step_size, rate, stretches)


def reduce_kernel(
    hid_ref, cols_ref, few_ref, out_ref, total_ref,
    hid, prod, mate_out, mate_in, a_out, a_own, a_in, a2_out, a2_own, a2_in,
    b_out, b_own, b_in, b2_out, b2_own, b2_in, few, few_c, few_z, few_x, load_sem, ss, rs,
):
    x, z, c, head = place()
    load = pltpu.make_async_copy(hid_ref, hid, load_sem)
    load.start()
    greet(plane_partners(x, z, c, head))
    mate = at(x, z, 1 - c, head)
    started = []

    def send(source, target, k, partner):
        copy = pltpu.make_async_remote_copy(
            source, target, ss.at[k], rs.at[k], device_id=partner, device_id_type=MESH
        )
        copy.start()
        started.append(copy)
        return copy

    few[0] = few_ref[...]
    few_copy = send(few.at[0], few_c, 0, mate)
    load.wait()
    grads = cols_ref[...]
    span = MODEL // NX
    order = (2, 1, 3, 0)
    mate_copies = {}
    for dx in order:
        to = (x + dx) % NX
        chunk = hid[:, pl.ds(pl.multiple_of(to * span, span), span)]
        prod[dx] = dot(chunk, grads, ((0,), (0,))).reshape(NZ, NC, DEPTH, COLS)
        mate_out[dx] = prod[dx, :, 1 - c].astype(BF16)
        mate_copies[dx] = send(mate_out.at[dx], mate_in.at[dx], 1 + dx, mate)
    few_copy.wait_recv()
    few[1] = few[0] + few_c[...]
    few_copies = [
        send(few.at[1], few_z.at[dz - 1], 4 + dz, at(x, z + dz, c, head)) for dz in range(1, NZ)
    ]
    a_copies = []
    for dx in order:
        mate_copies[dx].wait_recv()
        chip = prod[dx, :, c] + mate_in[dx].astype(F32)
        b_own[dx] = chip[:, PART:]
        b_out[:, dx] = chip[:, PART:].astype(BF16)
        if dx:
            a_out[dx - 1] = chip[:, :PART].astype(BF16)
            a_copies.append(send(a_out.at[dx - 1], a_in.at[dx - 1], 11 + dx, at(x + dx, z, c, head)))
        else:
            a_own[...] = chip[:, :PART]
    b_copies = [
        send(b_out.at[(z + dz) % NZ], b_in.at[dz - 1], 14 + dz, at(x, z + dz, c, head))
        for dz in (4, 3, 5, 2, 6, 1, 7)
    ]
    for copy in few_copies:
        copy.wait_recv()
    few[2] = few[1] + jnp.sum(few_z[...], axis=0)
    few_copies = [
        send(few.at[2], few_x.at[dx - 1], 21 + dx, at(x + dx, z, c, head)) for dx in range(1, NX)
    ]
    for copy in b_copies:
        copy.wait_recv()
    b2_own[...] = b_own[:, z] + jnp.sum(b_in[...].astype(F32), axis=0)
    b2_out[...] = b2_own[...].astype(BF16)
    b2_copies = [
        send(b2_out.at[dx], b2_in.at[dx - 1], 24 + dx, at(x + dx, z, c, head)) for dx in range(1, NX)
    ]
    for copy in a_copies:
        copy.wait_recv()
    a2_own[...] = a_own[...] + jnp.sum(a_in[...].astype(F32), axis=0)
    a2_out[...] = a2_own[...].astype(BF16)
    a2_copies = [
        send(a2_out.at[(z + dz) % NZ], a2_in.at[dz - 1], 27 + dz, at(x, z + dz, c, head))
        for dz in (4, 3, 5, 2, 6, 1, 7)
    ]
    for copy in few_copies + b2_copies:
        copy.wait_recv()
    total_ref[...] = few[2] + jnp.sum(few_x[...], axis=0)
    out_ref[PART:] = b2_own[0] + jnp.sum(b2_in[...].astype(F32), axis=0)
    for copy in a2_copies:
        copy.wait_recv()
    out_ref[:PART] = a2_own[z] + jnp.sum(a2_in[...].astype(F32), axis=0)
    for copy in started:
        copy.wait_send()


def reduce_part(hidden, grad_cols, few):
    vmem = pl.BlockSpec(memory_space=pltpu.VMEM)
    shape = jax.ShapeDtypeStruct
    rest = DEPTH - PART
    return pl.pallas_call(
        reduce_kernel,
        name="reduce_part",
        out_shape=(shape((DEPTH, COLS), F32), shape((8, 128), F32)),
        in_specs=[pl.BlockSpec(memory_space=pl.ANY), vmem, vmem],
        out_specs=(vmem, vmem),
        scratch_shapes=[
            pltpu.VMEM((TOK, MODEL), BF16),
            pltpu.VMEM((NX, NZ, NC, DEPTH, COLS), F32),
            pltpu.VMEM((NX, NZ, DEPTH, COLS), BF16),
            pltpu.VMEM((NX, NZ, DEPTH, COLS), BF16),
            pltpu.VMEM((NX - 1, NZ, PART, COLS), BF16),
            pltpu.VMEM((NZ, PART, COLS), F32),
            pltpu.VMEM((NX - 1, NZ, PART, COLS), BF16),
            pltpu.VMEM((NZ, PART, COLS), BF16),
            pltpu.VMEM((NZ, PART, COLS), F32),
            pltpu.VMEM((NZ - 1, PART, COLS), BF16),
            pltpu.VMEM((NZ, NX, rest, COLS), BF16),
            pltpu.VMEM((NX, NZ, rest, COLS), F32),
            pltpu.VMEM((NZ - 1, NX, rest, COLS), BF16),
            pltpu.VMEM((NX, rest, COLS), BF16),
            pltpu.VMEM((NX, rest, COLS), F32),
            pltpu.VMEM((NX - 1, rest, COLS), BF16),
            pltpu.VMEM((3, 8, 128), F32),
            pltpu.VMEM((8, 128), F32),
            pltpu.VMEM((NZ - 1, 8, 128), F32),
            pltpu.VMEM((NX - 1, 8, 128), F32),
            pltpu.SemaphoreType.DMA,
            pltpu.SemaphoreType.DMA((35,)),
            pltpu.SemaphoreType.DMA((35,)),
        ],
        compiler_params=pltpu.CompilerParams(
            collective_id=2, has_side_effects=True, vmem_limit_bytes=VMEM_LIMIT
        ),
    )(hidden, grad_cols, few)


def body(
    hidden, w_bc, x_act, step_size, decay_rate, skip_gain, logp_dir, base_logp, seq_stretches, resp_mask
):
    bc, dec = gather(w_bc, step_size, decay_rate, hidden)
    msg, tab, own, gbc, gx, rows, cols, xf, dyg, small = local_part(
        bc, x_act, logp_dir, step_size, resp_mask.reshape(1, TOK), base_logp.reshape(1, TOK), dec,
        decay_rate, skip_gain, seq_stretches,
    )
    states, sums = scan_part(msg, tab, own)
    grad_x, grad_step, grad_cols, few = grad_part(
        states, sums, bc, x_act, xf, dyg, gbc, gx, rows, cols, small, step_size, decay_rate, seq_stretches
    )
    grad_w, total = reduce_part(hidden, grad_cols, few)
    return grad_x, grad_step, total[0, :HEADS], total[1, :HEADS], grad_w


def solution(mesh):
    return jax.shard_map(
        body,
        mesh=mesh,
        in_specs=(
            P("ctx", None),
            P("ctx", "head"),
            P("ctx", "head"),
            P("head", "ctx"),
            P("head"),
            P("head"),
            P("ctx", "head"),
            P("ctx"),
            P(),
            P("ctx"),
        ),
        out_specs=(P("ctx", "head"), P("head", "ctx"), P("head"), P("head"), P("ctx", "head")),
        check_vma=False,
    )
```

time: 771 us -> 108 us (0.14); the launches traced: 762 us -> 107 us
  blocking collectives: 301 us -> 0 us
  waiting for transfers between devices: 206 us -> 0 us
  other arithmetic: 156 us -> 0 us
  Pallas kernels: 0 us -> 102 us
  local copies, waits for them, and re-layouts: 55.6 us -> 4.91 us
  matrix products: 21.5 us -> 0 us
  between operations: 17.3 us -> 0.78 us
    psum x2 -> x0, blocking collectives: 220 us -> none  [the longest x1 124 us: body(): lax.psum((grad_rate_local.reshape(head_count), grad_skip_local.reshape(he...]
    all_gather x3 -> x0, waiting for transfers between devices: 200 us -> none  [the longest x2 115 us: prefix(): everything = jax.tree.map(lambda part: lax.all_gather(part, axis), x)]
    select_n x128 -> x0, other arithmetic: 135 us -> none  [hop(): return jax.tree.map(lambda a, b: jnp.where(reached, a, b), new, before)]
    pallas_call x0 -> x5, Pallas kernels: none -> 102 us  [the longest x1 37.6 us: scan_part(): pl.pallas_call(scan_kernel, name='scan_part', out_shape=(shape((NCTX, 16,...]
    all_gather x2 -> x0, blocking collectives: 81.1 us -> none  [prefix(): everything = jax.tree.map(lambda part: lax.all_gather(part, axis), x)]
    mul x130 -> x0, local copies, waits for them, and re-layouts: 42.9 us -> none  [the longest x128 41.5 us: chain_pair(): later_part[0][:, :, None, None] * earlier[1] + later_part[1]]
    dot_general x14 -> x0, matrix products: 21.5 us -> none  [the longest x9 13.6 us: einsum_wide(): return jnp.einsum(form, left, right, preferred_element_type=jnp.float32)]
    reduce_sum x9 -> x0, other arithmetic: 7.88 us -> none  [the longest x2 2.08 us: block_output(): skip_group[None, :, :, None] * inputs.astype(jnp.float32)]
  transfers between devices with their start and end apart: 4 -> 0, of which waited for: 4 -> 0; matrix products, arithmetic and copies ran while one was open for 4% -> 0% of each run, Pallas kernels for 0% -> 0%
where the time goes in v1:
time: 108 us; the launch traced here: 107 us
  Pallas kernels  102 us (94%)
  local copies, waits for them, and re-layouts  4.91 us (5%)
    pallas_call x1, Pallas kernels, scan_part(): pl.pallas_call(scan_kernel, name='scan_part', out_shape=(shape((NCTX, 16,...  37.6 us
    pallas_call x1, Pallas kernels, gather(): pl.pallas_call(gather_kernel, name='gather_project', out_shape=(jax.Shape...  32.7 us
    pallas_call x1, Pallas kernels, reduce_part(): pl.pallas_call(reduce_kernel, name='reduce_part', out_shape=(shape((DEPTH...  24.4 us
    unnamed x27, local copies, waits for them, and re-layouts  4.39 us
    pallas_call x1, Pallas kernels, local_part(): pl.pallas_call(local_kernel, name='local_part', out_shape=(shape((NCTX, 1...  4.18 us
    pallas_call x1, Pallas kernels, grad_part(): pl.pallas_call(grad_kernel, name='grad_part', out_shape=(shape((TOK, WIDE...  2.91 us

profile of v1, /device:TPU:1, one launch (start us, length us, event | category | flops | bytes accessed | tf_op | source)
XLA Modules:
  0.0 107.5 jit_solution(8510773841153740578)
XLA Ops:
  0.6 0.0 copy-start.8
  0.6 0.0 copy-start.9
  0.7 0.0 copy-start.10
  0.7 0.0 copy-start.11
  0.7 0.0 copy-start.12
  0.7 0.0 copy-start
  0.7 1.6 %copy-done = bf16[256,4096]{1,0:T(8,128)(2,1)S(1)} copy-done((bf16[256,4096]{1,0:T(8,128)(2,1)S(1)}, bf16[256,4096]{1,0:T(8,128)(2,1)}, u32[]{:S(2)}) %copy-start) | copy-done | bytes 2097176
  2.3 0.7 copy-done.4
  3.0 0.8 copy-done.6
  3.8 0.7 copy-done.7
  4.4 32.7 %gather_project.1 = (bf16[256,256]{1,0:T(8,128)(2,1)S(1)}, f32[4,8,2,1,128]{4,3,2,1,0:T(1,128)S(1)}) custom-call(bf16[64,256]{1,0:T(8,128)(2,1)S(1)} %copy-done.6, f32[8,256]{1,0:T(8,128)S(1)} %copy-done.4, f32[8]{0:T(128)S(1)} %copy-done.7, bf16[256,4096]{1,0:T(8,128)(2,1)S(1)} %copy-done), custom_call_target="tpu_custom_call" | custom-call | tf_op jit(solution)/shard_map/gather_project/pallas_call | solution.py:136
  37.1 0.0 copy-start.1
  37.2 0.0 copy-done.8
  37.2 0.0 copy-done.9
  37.2 0.0 copy-done.10
  37.2 0.0 copy-done.11
  37.2 0.0 copy-done.12
  37.2 0.0 copy-done.2
  37.2 4.2 %local_part.1 = (bf16[64,16,128]{2,1,0:T(8,128)(2,1)S(1)}, f32[7,64,128]{2,1,0:T(8,128)S(1)}, f32[8,128]{1,0:T(8,128)S(1)}, f32[256,256]{1,0:T(8,128)S(1)}, f32[...) custom-call(bf16[256,256]{1,0:T(8,128)(2,1)S(1)} %get-tuple-element., ...), custom_call_target="tpu_custom_call" | custom-call | tf_op jit(solution)/shard_map/local_part/pallas_call | solution.py:288
  41.4 37.6 %scan_part.1 = (bf16[64,16,128]{2,1,0:T(8,128)(2,1)S(1)}, f32[8,128]{1,0:T(8,128)S(1)}) custom-call(bf16[64,16,128]{2,1,0:T(8,128)(2,1)S(1)} %get-tuple-element.27.msg_ref, f32[7,64,128]{2,1,0:T(8,128)S(1)} %get-tuple-element.28.tab_ref, f32[8,128]{1,0:T(8,128)S(1)} %get-tuple-element.29.own_ref), custom_call_target="tpu_custom_call" | custom-call | tf_op jit(solution)/shard_map/scan_part/pallas_call | solution.py:423
  79.0 2.9 %grad_part.1 = (bf16[256,512]{1,0:T(8,128)(2,1)}, f32[8,256]{1,0:T(8,128)}, bf16[256,256]{1,0:T(8,128)(2,1)S(1)}, f32[8,128]{1,0:T(8,128)S(1)}) custom-call(bf16[64,16,128]{2,1,0:T(8,128)(2,1)S(1)} %get-tuple-element.30.states_ref, f32[8,128]{1,0:T(8,128)S(1)} %get-tuple-element.31.sums_ref, bf16[256,256]{1,0:T(8,128)(2,1)S(1)} %get-tuple-element.25.bc_ref, ...), custom_call_target="tpu_custom_call" | custom-call | tf_op jit(solution)/shard_map/grad_part/pallas_call | solution.py:523
  81.9 24.4 %reduce_part.1 = (f32[64,256]{1,0:T(8,128)S(1)}, f32[8,128]{1,0:T(8,128)S(1)}) custom-call(bf16[256,4096]{1,0:T(8,128)(2,1)S(1)} %copy-done.1, bf16[256,256]{1,0:T(8,128)(2,1)S(1)} %get-tuple-element.41.cols_ref, f32[8,128]{1,0:T(8,128)S(1)} %get-tuple-element.42.few_ref), custom_call_target="tpu_custom_call" | custom-call | tf_op jit(solution)/shard_map/reduce_part/pallas_call | solution.py:627
  106.3 0.5 slice_bitcast_fusion
  106.8 0.6 copy.16
  (9 shorter events, 0.0 us)
Async XLA Ops:
  0.6 36.5 %copy-start.8 = (f32[8]{0:T(128)S(1)}, f32[8]{0:T(128)}, u32[]{:S(2)}) copy-start(f32[8]{0:T(128)} %rate_ref.5) | copy-start | bytes 100
  0.6 36.5 %copy-start.9 = (s32[4]{0:T(128)S(1)}, s32[4]{0:T(128)}, u32[]{:S(2)}) copy-start(s32[4]{0:T(128)} %stretch_ref.3) | copy-start | bytes 52
  0.7 36.5 %copy-start.10 = (s32[256]{0:T(256)S(1)}, s32[256]{0:T(256)}, u32[]{:S(2)}) copy-start(s32[256]{0:T(256)} %param.19) | copy-start | bytes 3076
  0.7 36.5 %copy-start.11 = (f32[256]{0:T(256)S(1)}, f32[256]{0:T(256)}, u32[]{:S(2)}) copy-start(f32[256]{0:T(256)} %param.17) | copy-start | bytes 3076
  0.7 36.5 %copy-start.12 = (f32[8]{0:T(128)S(1)}, f32[8]{0:T(128)}, u32[]{:S(2)}) copy-start(f32[8]{0:T(128)} %skip_ref.1) | copy-start | bytes 100
  0.7 1.6 %copy-start = (bf16[256,4096]{1,0:T(8,128)(2,1)S(1)}, bf16[256,4096]{1,0:T(8,128)(2,1)}, u32[]{:S(2)}) copy-start(bf16[256,4096]{1,0:T(8,128)(2,1)} %hid_ref.3) | copy-start | bytes 6291460
  2.3 0.7 copy-start.4
  3.0 0.8 copy-start.6
  3.8 0.7 copy-start.7
  4.4 32.8 %copy-start.2 = (bf16[256,512]{1,0:T(8,128)(2,1)S(1)}, bf16[256,512]{1,0:T(8,128)(2,1)}, u32[]{:S(2)}) copy-start(bf16[256,512]{1,0:T(8,128)(2,1)} %x_ref.3) | copy-start | bytes 786436
  4.4 32.8 %copy-start.3 = (bf16[256,512]{1,0:T(8,128)(2,1)S(1)}, bf16[256,512]{1,0:T(8,128)(2,1)}, u32[]{:S(2)}) copy-start(bf16[256,512]{1,0:T(8,128)(2,1)} %dir_ref.1) | copy-start | bytes 786436
  4.4 32.8 %copy-start.5 = (f32[8,256]{1,0:T(8,128)S(1)}, f32[8,256]{1,0:T(8,128)}, u32[]{:S(2)}) copy-start(f32[8,256]{1,0:T(8,128)} %step_ref.5) | copy-start | bytes 24580
  37.1 44.8 %copy-start.1 = (bf16[256,4096]{1,0:T(8,128)(2,1)S(1)}, bf16[256,4096]{1,0:T(8,128)(2,1)}, u32[]{:S(2)}) copy-start(bf16[256,4096]{1,0:T(8,128)(2,1)} %hid_ref.3) | copy-start | bytes 6291460

commit v2 on v1

v2 whole, which is shorter than its diff:
```python
import functools

import jax
import jax.numpy as jnp
from jax import lax
from jax.experimental import pallas as pl
from jax.experimental.pallas import tpu as pltpu
from jax.sharding import PartitionSpec as P

HEADDIM = 64
NSTATE = 128
NX, NZ, NC = 4, 8, 2
NCTX = NX * NZ * NC
CHIPS = NX * NZ
NHEAD = 8
TOK = 256
HEADS = 8
WIDE = HEADS * HEADDIM
DEPTH = 64
COLS = 2 * NSTATE
MODEL = NCTX * DEPTH
PART = 48

hinge_sharp = 0.005
hinge_margin = 10.0

MESH = pl.DeviceIdType.MESH
F32 = jnp.float32
BF16 = jnp.bfloat16
VMEM_LIMIT = 48 << 20
SPACE = pltpu.HBM


def place():
    index = lax.axis_index("ctx")
    return index // 16, (index // 2) % 8, index % 2, lax.axis_index("head")


def at(x, z, c, head):
    return (((x % NX) * NZ + (z % NZ)) * NC + c, head)


def greet(partners):
    barrier = pltpu.get_barrier_semaphore()
    for partner in partners:
        pl.semaphore_signal(barrier, inc=1, device_id=partner, device_id_type=MESH)
    pl.semaphore_wait(barrier, len(partners))


def plane_partners(x, z, c, head):
    return (
        [at(x, z + dz, c, head) for dz in range(1, NZ)]
        + [at(x + dx, z, c, head) for dx in range(1, NX)]
        + [at(x, z, 1 - c, head)]
    )


def dot(left, right, dims=((1,), (0,)), precision=None):
    return lax.dot_general(left, right, (dims, ((), ())), precision=precision, preferred_element_type=F32)


def pair_columns(columns, base, pair, low_half):
    one, two = base + 2 * pair, base + 2 * pair + 1
    return jnp.where(low_half, columns[:, one : one + 1], columns[:, two : two + 1])


def sequence_starts(stretch_ref):
    one = stretch_ref[0]
    two = one + stretch_ref[1]
    return one, two, two + stretch_ref[2]


def halves(value):
    top = value.astype(BF16)
    return top, (value - top.astype(F32)).astype(BF16)


def keep_of(block, starts):
    begins = block == 0
    for start in starts:
        begins = begins | (block == start)
    return jnp.where(begins, 0.0, 1.0)


def seq_of(block, starts):
    return sum((block >= start).astype(jnp.int32) for start in starts)


def front_kernel(
    hid_hbm, w_hbm, x_hbm, dir_hbm, step_hbm, rate_hbm, skip_hbm, mask_hbm, base_hbm, stretch_hbm,
    gx_ref, gstep_ref, gcols_ref, few_ref, sums_ref,
    hid, x_ref, dir_ref, step_ref, rate_ref, skip_ref, mask_ref, base_ref, stretch_ref,
    buf, dec, factors, moves, stack, cols_ref, xf_ref, dyg_ref, drow, dcol, lg, mate_lg, msg, got, wide,
    swept, reply, states, tab, part, near, across,
    load_sem, send_sem, recv_sem, ss, rs, gs, gr,
):
    index = lax.axis_index("ctx")
    x, z, c, head = place()
    chip = index // 2
    mate = at(x, z, 1 - c, head)
    every = slice(None)

    loads = {}
    for k, (name, source, target) in enumerate(
        (
            ("step", step_hbm, step_ref),
            ("rate", rate_hbm, rate_ref),
            ("w", w_hbm, buf.at[x, z, c]),
            ("mask", mask_hbm, mask_ref),
            ("x", x_hbm, x_ref),
            ("dir", dir_hbm, dir_ref),
            ("skip", skip_hbm, skip_ref),
            ("base", base_hbm, base_ref),
            ("stretch", stretch_hbm, stretch_ref),
            ("hid", hid_hbm, hid),
        )
    ):
        loads[name] = pltpu.make_async_copy(source, target, load_sem.at[k])
        loads[name].start()

    barrier = pltpu.get_barrier_semaphore()

    def hello(k, carry):
        to = (chip + k) % CHIPS
        pl.semaphore_signal(barrier, inc=1, device_id=(to * 2 + c, head), device_id_type=MESH)
        return carry

    def hello_head(k, carry):
        to = (head + k // 2) % NHEAD
        who = chip * 2 + (c + k) % 2
        pl.semaphore_signal(barrier, inc=1, device_id=(who, to), device_id_type=MESH)
        return carry

    lax.fori_loop(1, CHIPS, hello, 0)
    lax.fori_loop(1, 2 * NHEAD, hello_head, 0)
    loads["w"].wait()
    pl.semaphore_wait(barrier, CHIPS - 1 + 2 * NHEAD - 1)

    started, slots = [], {}

    def slot(key):
        return slots.setdefault(key, len(slots))

    def send(ref, where, key, partner, into=None):
        k = slot(key)
        copy = pltpu.make_async_remote_copy(
            ref.at[where],
            (ref if into is None else into).at[where],
            ss.at[k],
            rs.at[k],
            device_id=partner,
            device_id_type=MESH,
        )
        copy.start()
        started.append(copy)

    def arrive(ref, where, key):
        piece = ref.at[where]
        k = slot(key)
        pltpu.make_async_remote_copy(
            piece, piece, ss.at[k], rs.at[k], device_id=mate, device_id_type=MESH
        ).wait_recv()

    low, high = pl.ds(0, PART), pl.ds(PART, DEPTH - PART)
    near_z, near_x = (1, 7, 2, 6, 3, 5, 4), (1, 3, 2)

    def to_z(dz):
        return at(x, z + dz, c, head)

    def to_x(dx):
        return at(x + dx, z, c, head)

    def from_z(dz):
        return (z - dz) % NZ

    def from_x(dx):
        return (x - dx) % NX

    for dz in near_z:
        send(buf, (x, z, c, low), ("az", dz), to_z(dz))
    for dx in near_x:
        send(buf, (x, z, c, high), ("bx", dx), to_x(dx))
    for dx in near_x:
        send(buf, (x, z, c, low), ("ax", 0, dx), to_x(dx))
    for dz in near_z:
        send(buf, (x, z, c, high), ("bz", 0, dz), to_z(dz))
    send(buf, (x, z, c), ("own",), mate)

    loads["step"].wait()
    loads["rate"].wait()
    rows8 = lax.broadcasted_iota(jnp.int32, (8, 128), 0)
    lanes8 = lax.broadcasted_iota(jnp.int32, (8, 128), 1)
    step = step_ref[...]
    row8 = lax.broadcasted_iota(jnp.int32, (8, TOK), 0)
    rate = jnp.zeros((8, TOK), F32)
    for h in range(HEADS):
        rate = jnp.where(row8 == h, rate_ref[h], rate)
    total = -rate[:, 0:1] * jnp.sum(step, axis=1, keepdims=True)
    dec[x, z, c] = jnp.sum(jnp.where(rows8 == lanes8, total, 0.0), axis=0, keepdims=True)
    for dz in near_z:
        send(dec, (x, z, c), ("dz", dz), to_z(dz))

    s_index = lax.broadcasted_iota(jnp.int32, (TOK, TOK), 0)
    t_index = lax.broadcasted_iota(jnp.int32, (TOK, TOK), 1)
    causal = s_index <= t_index
    cum = -rate * dot(step, causal.astype(F32), precision=lax.Precision.HIGHEST)
    last = cum[:, TOK - 1 : TOK]
    loads["mask"].wait()
    mask = mask_ref[...].astype(F32)
    stack[...] = jnp.zeros((128, TOK), F32)
    stack[0:8] = cum - jnp.log(step)
    stack[8:16] = jnp.exp(cum)
    stack[16:24] = jnp.exp(last - cum) * step
    stack[24:32] = jnp.broadcast_to(mask, (8, TOK))
    columns = stack[...].T
    cols_ref[...] = columns
    loads["x"].wait()
    loads["dir"].wait()
    loads["skip"].wait()
    loads["base"].wait()
    loads["stretch"].wait()
    low_half = lax.broadcasted_iota(jnp.int32, (TOK, 128), 1) < HEADDIM
    overlap = []

    def prepare(pair):
        columns = cols_ref[...]
        span = slice(128 * pair, 128 * pair + 128)
        x_pair = x_ref[:, span]
        x_wide = x_pair.astype(F32)
        dy_wide = dir_ref[:, span].astype(F32) * columns[:, 24:25]
        dy_pair = dy_wide.astype(BF16)
        dir_ref[:, span] = dy_pair
        xf_ref[:, span] = (x_wide * pair_columns(columns, 16, pair, low_half)).astype(BF16)
        dyg_ref[:, span] = (dy_wide * pair_columns(columns, 8, pair, low_half)).astype(BF16)
        overlap.append(jnp.sum(x_wide * dy_wide, axis=0, keepdims=True))
        for h in (2 * pair, 2 * pair + 1):
            half = slice(HEADDIM * (h % 2), HEADDIM * (h % 2) + HEADDIM)
            gap = jnp.where(causal, cum[h : h + 1, :] - columns[:, h : h + 1], -1e30)
            factor = jnp.exp(gap)
            factors[h] = factor
            moves[h] = dot(x_pair[:, half], dy_pair[:, half], ((1,), (1,))) * factor
        skip_pair = jnp.where(low_half, skip_ref[2 * pair], skip_ref[2 * pair + 1])
        gx_ref[:, span] = skip_pair * dy_wide

    def forward_low(dz):
        where = (x, from_z(dz), c, low)
        arrive(buf, where, ("az", dz))
        for dx in near_x:
            send(buf, where, ("ax", dz, dx), to_x(dx))
        send(buf, where, ("am", dz), mate)

    def forward_high(dx):
        where = (from_x(dx), z, c, high)
        arrive(buf, where, ("bx", dx))
        for dz in near_z:
            send(buf, where, ("bz", dx, dz), to_z(dz))
        send(buf, where, ("bm", dx), mate)

    def take_low(dz, dx):
        where = (from_x(dx), from_z(dz), c, low)
        arrive(buf, where, ("ax", dz, dx))
        send(buf, where, ("axm", dz, dx), mate)

    def take_high(dz):
        for dx in (0, 1, 3, 2):
            arrive(buf, (from_x(dx), from_z(dz), c, high), ("bz", dx, dz))
        send(buf, (every, from_z(dz), c, high), ("bzm", dz), mate)

    prepare(0)
    for dz in (1, 7):
        forward_low(dz)
    for dx in (1, 3):
        forward_high(dx)
    prepare(1)
    for dz in (2, 6):
        forward_low(dz)
    forward_high(2)
    prepare(2)
    for dz in (3, 5, 4):
        forward_low(dz)
    for dz in near_z:
        arrive(dec, (x, from_z(dz), c), ("dz", dz))
    for dx in near_x:
        send(dec, (x, every, c), ("dx", dx), to_x(dx))
    prepare(3)
    for dx in near_x:
        take_low(0, dx)
    for dz in (1, 7):
        for dx in near_x:
            take_low(dz, dx)
    for dz in (1, 7):
        take_high(dz)
    for dz in (2, 6):
        for dx in near_x:
            take_low(dz, dx)
    for dz in (2, 6):
        take_high(dz)
    for dx in near_x:
        arrive(dec, (from_x(dx), every, c), ("dx", dx))
    send(dec, (every, every, c), ("dm",), mate)
    for dz in (3, 5, 4):
        for dx in near_x:
            take_low(dz, dx)
        take_high(dz)

    other = 1 - c
    arrive(buf, (x, z, other), ("own",))
    for dz in near_z:
        arrive(buf, (x, from_z(dz), other, low), ("am", dz))
    for dx in near_x:
        arrive(buf, (from_x(dx), z, other, high), ("bm", dx))
    for dz in (0,) + near_z:
        for dx in near_x:
            arrive(buf, (from_x(dx), from_z(dz), other, low), ("axm", dz, dx))
    for dz in near_z:
        arrive(buf, (every, from_z(dz), other, high), ("bzm", dz))
    loads["hid"].wait()
    span = MODEL // NX
    sums = jnp.zeros((TOK, COLS), F32)
    for k in range(NX):
        sums = sums + dot(hid[:, k * span : (k + 1) * span], buf[k].reshape(span, COLS))
    bc = sums.astype(BF16)
    b_in, c_in = bc[:, :NSTATE], bc[:, NSTATE:]
    lg[0] = dot(xf_ref[...], b_in, ((0,), (0,))).reshape(2, WIDE // 2, NSTATE)
    lg[1] = dot(dyg_ref[...], c_in, ((0,), (0,))).reshape(2, WIDE // 2, NSTATE)
    send(lg, (every, other), ("l1",), mate, mate_lg)
    send(lg, (every, c), ("l2",), mate, mate_lg)

    starts = sequence_starts(stretch_ref)
    arrive(dec, (every, every, other), ("dm",))
    row0, row1 = jnp.exp(dec[x, z, 0]), jnp.exp(dec[x, z, 1])
    lane1 = lax.broadcasted_iota(jnp.int32, (1, 128), 1)

    def pick(row, h):
        return jnp.sum(jnp.where(lane1 == h, row, 0.0), axis=1, keepdims=True)

    keep0, keep1 = keep_of(2 * chip, starts), keep_of(2 * chip + 1, starts)
    next1 = jnp.where(2 * chip + 2 == NCTX, 0.0, keep_of(2 * chip + 2, starts))
    first = c == 0
    arrive(mate_lg, (every, c), ("l1",))
    met = jnp.zeros((HEADDIM, 128), F32)
    chip_l, chip_g = [], []
    for hh in range(HEADS // 2):
        span = slice(HEADDIM * hh, HEADDIM * hh + HEADDIM)
        mine_l, mine_g = lg[0, c, span], lg[1, c, span]
        mate_l, mate_g = mate_lg[0, c, span], mate_lg[1, c, span]
        l0, l1 = jnp.where(first, mine_l, mate_l), jnp.where(first, mate_l, mine_l)
        g0, g1 = jnp.where(first, mine_g, mate_g), jnp.where(first, mate_g, mine_g)
        h = 4 * c + hh
        chip_l.append(pick(row1, h) * keep1 * l0 + l1)
        chip_g.append(pick(row0, h) * keep1 * g1 + g0)
        met = met + l0 * g1
    msg[...] = jnp.concatenate(
        [
            jnp.concatenate(chip_l, axis=0).reshape(CHIPS, 8, 128),
            jnp.concatenate(chip_g, axis=0).reshape(CHIPS, 8, 128),
        ],
        axis=1,
    ).astype(BF16)

    def exchange(source, target, phase):
        def start(k, carry):
            to = (chip + k) % CHIPS
            pltpu.make_async_remote_copy(
                source.at[to],
                target.at[chip],
                send_sem.at[phase],
                recv_sem.at[phase],
                device_id=(to * 2 + c, head),
                device_id_type=MESH,
            ).start()
            return carry

        lax.fori_loop(1, CHIPS, start, 0)

    def settle(target, sem):
        rest = target.at[pl.ds(0, CHIPS - 1)]
        pltpu.make_async_copy(rest, rest, sem).wait()

    exchange(msg, got, 0)
    got[chip] = msg[chip]

    scores = dot(b_in, c_in, ((1,), (1,)))
    grad_scores = jnp.zeros((TOK, TOK), F32)
    back = jnp.zeros((TOK, 128), F32)
    lane128 = lax.broadcasted_iota(jnp.int32, (TOK, 128), 1)
    for pair in range(HEADS // 2):
        span = slice(128 * pair, 128 * pair + 128)
        within = []
        for h in (2 * pair, 2 * pair + 1):
            moved = moves[h]
            grad_scores = grad_scores + moved
            spent = moved * scores
            drow[h : h + 1] = jnp.sum(spent, axis=0, keepdims=True)
            back = jnp.where(lane128 == h, jnp.sum(spent, axis=1, keepdims=True), back)
            dy_h = dir_ref[:, HEADDIM * h : HEADDIM * h + HEADDIM]
            within.append(dot((scores * factors[h]).astype(BF16), dy_h))
        gx_ref[:, span] = gx_ref[:, span] + jnp.concatenate(within, axis=1)
    dcol[...] = back.T[0:8]
    grad_bf = grad_scores.astype(BF16)
    gcols_ref[:, :NSTATE] = dot(grad_bf, c_in)
    gcols_ref[:, NSTATE:] = dot(grad_bf, b_in, ((0,), (0,)))

    wide_row = lax.broadcasted_iota(jnp.int32, (WIDE, 128), 0) // HEADDIM
    wide_lane = lax.broadcasted_iota(jnp.int32, (WIDE, 128), 1)
    overlap_row = jnp.broadcast_to(jnp.concatenate(overlap, axis=1), (8, WIDE))
    overlap_head = dot(overlap_row, (wide_row == wide_lane).astype(F32), precision=lax.Precision.HIGHEST)
    few_ref[...] = overlap_head
    skip_row = jnp.zeros((1, 128), F32)
    for h in range(HEADS):
        skip_row = jnp.where(lane1 == h, skip_ref[h], skip_row)
    pieces = jnp.sum(grad_scores * scores, axis=0, keepdims=True)
    pieces = pieces + jnp.where(head == 0, 1.0, 0.0) * mask * base_ref[...]
    own = pieces[:, :128] + pieces[:, 128:] + overlap_head[0:1] * skip_row
    own = jnp.sum(own, axis=1, keepdims=True)
    pair_sum = keep1 * jnp.sum(jnp.sum(met, axis=0, keepdims=True), axis=1, keepdims=True)
    mine = jnp.where(lane1 == seq_of(index, starts), own, 0.0)
    mine = mine + jnp.where(lane1 == seq_of(2 * chip + 1, starts), pair_sum, 0.0)

    chips = lax.broadcasted_iota(jnp.int32, (CHIPS, 128), 0)
    lane32 = lax.broadcasted_iota(jnp.int32, (CHIPS, 128), 1)
    my_head = 4 * c + chip // 8

    def decays(core):
        table = jnp.concatenate([dec[m // NZ, m % NZ, core] for m in range(CHIPS)], axis=0)
        return jnp.exp(jnp.sum(jnp.where(lane32 == my_head, table, 0.0), axis=1, keepdims=True))

    both = decays(0) * decays(1) * keep_of(2 * chips + 1, starts)
    enters = keep_of(2 * chips, starts)
    tab[0] = both * enters
    tab[1] = both * jnp.where(chips == CHIPS - 1, 0.0, keep_of(2 * chips + 2, starts))

    settle(got, recv_sem.at[0])
    wide[...] = got[...].astype(F32)

    def advance(b, carry):
        state, grad = carry
        r = CHIPS - 1 - b
        swept[b, 0:8] = state
        swept[r, 8:16] = grad
        state = state * tab[0, pl.ds(b, 1)] + wide[b, 0:8]
        grad = grad * tab[1, pl.ds(r, 1)] + wide[r, 8:16]
        return state, grad

    zero = jnp.zeros((8, 128), F32)
    lax.fori_loop(0, CHIPS, advance, (zero, zero))
    reply[...] = swept[...].astype(BF16)
    exchange(reply, states.at[c], 1)
    states[c, chip] = reply[chip]

    met = jnp.sum(swept[:, 0:8] * wide[:, 8:16], axis=1) * enters
    met = jnp.sum(met, axis=1, keepdims=True)
    seqs = seq_of(2 * chips, starts)
    mine = mine + jnp.sum(jnp.where(lane32 == seqs, met, 0.0), axis=0, keepdims=True)
    part[0] = mine

    def spread(k, carry):
        to = (chip + k) % CHIPS
        pltpu.make_async_remote_copy(
            part.at[0], near.at[k], gs.at[0], gr.at[0], device_id=(to * 2 + c, head), device_id_type=MESH
        ).start()
        return carry

    lax.fori_loop(1, CHIPS, spread, 0)
    near[0] = mine

    def settle_few(target, sem, count):
        rest = target.at[pl.ds(1, count)]
        pltpu.make_async_copy(rest, rest, sem).wait()

    settle_few(near, gr.at[0], CHIPS - 1)
    gathered = jnp.sum(near[...], axis=0)
    part[1] = gathered

    def spread_head(k, carry):
        to = (head + k // 2) % NHEAD
        who = chip * 2 + (c + k) % 2
        pltpu.make_async_remote_copy(
            part.at[1], across.at[k], gs.at[1], gr.at[1], device_id=(who, to), device_id_type=MESH
        ).start()
        return carry

    lax.fori_loop(1, 2 * NHEAD, spread_head, 0)
    across[0] = gathered

    settle(states.at[c], recv_sem.at[1])
    send(states, (c,), ("st",), mate)
    arrive(mate_lg, (every, other), ("l2",))

    def spaced(row):
        return jnp.concatenate(
            [jnp.broadcast_to(pick(row, h), (HEADDIM, 128)) for h in range(HEADS)], axis=0
        )

    lead = jnp.where(first, keep0, keep0 * keep1 * spaced(row0))
    lead_mate = jnp.where(first, 0.0, keep1)
    trail = jnp.where(first, next1 * keep1 * spaced(row1), next1)
    trail_mate = jnp.where(first, keep1, 0.0)
    arrive(states, (other,), ("st",))
    states_f = states[...].astype(F32)
    state_in = lead * states_f[:, :, 0:8].reshape(WIDE, NSTATE)
    state_in = state_in + lead_mate * mate_lg[0].reshape(WIDE, NSTATE)
    grad_state = trail * states_f[:, :, 8:16].reshape(WIDE, NSTATE)
    grad_state = grad_state + trail_mate * mate_lg[1].reshape(WIDE, NSTATE)

    columns = cols_ref[...]
    state_bf, gstate_bf = state_in.astype(BF16), grad_state.astype(BF16)
    pick_half = lanes8 // HEADDIM
    nt = ((1,), (1,))
    carried = jnp.zeros((8, TOK), F32)
    kept = jnp.zeros((8, TOK), F32)
    for pair in range(HEADS // 2):
        span = slice(128 * pair, 128 * pair + 128)
        picks = (rows8 == 2 * pair + pick_half).astype(BF16)
        top, rest = halves(dot(c_in, state_bf[span], nt) * dyg_ref[:, span].astype(F32))
        carried = carried + dot(picks, top, nt) + dot(picks, rest, nt)
        pulled = dot(b_in, gstate_bf[span], nt) * pair_columns(columns, 16, pair, low_half)
        top, rest = halves(pulled * x_ref[:, span].astype(F32))
        kept = kept + dot(picks, top, nt) + dot(picks, rest, nt)
        gx_ref[:, span] = gx_ref[:, span] + pulled
    gcols_ref[:, :NSTATE] = gcols_ref[:, :NSTATE] + dot(xf_ref[...], gstate_bf)
    gcols_ref[:, NSTATE:] = gcols_ref[:, NSTATE:] + dot(dyg_ref[...], state_bf)

    grad_decay = jnp.sum(
        jnp.sum((state_in * grad_state).reshape(HEADS, HEADDIM, NSTATE), axis=1), axis=1, keepdims=True
    )
    end = jnp.sum(kept, axis=1, keepdims=True) + grad_decay * jnp.exp(last)
    token = lax.broadcasted_iota(jnp.int32, (8, TOK), 1)
    grad_cum = drow[...] - dcol[...] + carried - kept + jnp.where(token == TOK - 1, end, 0.0)
    tail = dot(grad_cum, (s_index >= t_index).astype(F32), precision=lax.Precision.HIGHEST)
    gstep_ref[...] = (dcol[...] + kept) / step - rate * tail
    grad_rate = -jnp.sum(step * tail, axis=1, keepdims=True)
    rate_row = jnp.sum(jnp.where(lanes8 == rows8, grad_rate, 0.0), axis=0, keepdims=True)
    few_ref[...] = jnp.where(rows8 == 0, rate_row, few_ref[...])

    settle_few(across, gr.at[1], 2 * NHEAD - 1)
    sums_ref[...] = jnp.broadcast_to(jnp.sum(across[...], axis=0), (8, 128))
    for copy in started:
        copy.wait_send()
    settle(msg, send_sem.at[0])
    settle(reply, send_sem.at[1])
    settle_few(near, gs.at[0], CHIPS - 1)
    settle_few(across, gs.at[1], 2 * NHEAD - 1)


def front(hidden, w_bc, x_act, logp_dir, step_size, rate, skip, mask, base, stretches):
    shape = jax.ShapeDtypeStruct
    vmem = pl.BlockSpec(memory_space=pltpu.VMEM)
    count = 120
    return pl.pallas_call(
        front_kernel,
        name="front",
        out_shape=(
            shape((TOK, WIDE), F32),
            shape((8, TOK), F32),
            shape((TOK, COLS), F32),
            shape((8, 128), F32),
            shape((8, 128), F32),
        ),
        in_specs=[pl.BlockSpec(memory_space=SPACE)] * 10,
        out_specs=tuple([vmem] * 5),
        scratch_shapes=[
            pltpu.VMEM((TOK, MODEL), BF16),
            pltpu.VMEM((TOK, WIDE), BF16),
            pltpu.VMEM((TOK, WIDE), BF16),
            pltpu.VMEM((8, TOK), F32),
            pltpu.SMEM((8,), F32),
            pltpu.SMEM((8,), F32),
            pltpu.VMEM((1, TOK), jnp.int32),
            pltpu.VMEM((1, TOK), F32),
            pltpu.SMEM((4,), jnp.int32),
            pltpu.VMEM((NX, NZ, NC, DEPTH, COLS), BF16),
            pltpu.VMEM((NX, NZ, NC, 1, 128), F32),
            pltpu.VMEM((HEADS, TOK, TOK), F32),
            pltpu.VMEM((HEADS, TOK, TOK), F32),
            pltpu.VMEM((128, TOK), F32),
            pltpu.VMEM((TOK, 128), F32),
            pltpu.VMEM((TOK, WIDE), BF16),
            pltpu.VMEM((TOK, WIDE), BF16),
            pltpu.VMEM((8, TOK), F32),
            pltpu.VMEM((8, TOK), F32),
            pltpu.VMEM((2, 2, WIDE // 2, NSTATE), F32),
            pltpu.VMEM((2, 2, WIDE // 2, NSTATE), F32),
            pltpu.VMEM((CHIPS, 16, 128), BF16),
            pltpu.VMEM((CHIPS, 16, 128), BF16),
            pltpu.VMEM((CHIPS, 16, 128), F32),
            pltpu.VMEM((CHIPS, 16, 128), F32),
            pltpu.VMEM((CHIPS, 16, 128), BF16),
            pltpu.VMEM((2, CHIPS, 16, 128), BF16),
            pltpu.VMEM((2, CHIPS, 128), F32),
            pltpu.VMEM((2, 1, 128), F32),
            pltpu.VMEM((CHIPS, 1, 128), F32),
            pltpu.VMEM((2 * NHEAD, 1, 128), F32),
            pltpu.SemaphoreType.DMA((10,)),
            pltpu.SemaphoreType.DMA((2,)),
            pltpu.SemaphoreType.DMA((2,)),
            pltpu.SemaphoreType.DMA((count,)),
            pltpu.SemaphoreType.DMA((count,)),
            pltpu.SemaphoreType.DMA((2,)),
            pltpu.SemaphoreType.DMA((2,)),
        ],
        compiler_params=pltpu.CompilerParams(
            collective_id=0, has_side_effects=True, vmem_limit_bytes=VMEM_LIMIT
        ),
    )(hidden, w_bc, x_act, logp_dir, step_size, rate, skip, mask, base, stretches)


def finish_kernel(gx_ref, gstep_ref, gcols_ref, few_ref, sums_ref, stretch_ref, grad_x_ref, grad_step_ref, cols_ref, small_ref):
    index = lax.axis_index("ctx")
    one, two, three = sequence_starts(stretch_ref)
    sums = sums_ref[0:1]
    lane = lax.broadcasted_iota(jnp.int32, (1, 128), 1)
    base = jnp.where(index >= two, 2, 0)
    signed = jnp.where(lane == base, sums, 0.0) - jnp.where(lane == base + 1, sums, 0.0)
    margin = jnp.sum(signed, axis=1, keepdims=True)
    coef = 1.0 / (1.0 + jnp.exp(-hinge_sharp * (hinge_margin - margin)))
    rejected = ((index >= one) & (index < two)) | (index >= three)
    scale = jnp.where(rejected, coef, -coef)
    grad_x_ref[...] = (gx_ref[...] * scale).astype(BF16)
    grad_step_ref[...] = gstep_ref[...] * scale
    cols_ref[...] = (gcols_ref[...] * scale).astype(BF16)
    small_ref[...] = few_ref[...] * scale


def finish(gx, gstep, gcols, few, sums, stretches):
    vmem = pl.BlockSpec(memory_space=pltpu.VMEM)
    shape = jax.ShapeDtypeStruct
    return pl.pallas_call(
        finish_kernel,
        name="finish",
        out_shape=(
            shape((TOK, WIDE), BF16),
            shape((8, TOK), F32),
            shape((TOK, COLS), BF16),
            shape((8, 128), F32),
        ),
        in_specs=[vmem] * 5 + [pl.BlockSpec(memory_space=pltpu.SMEM)],
        out_specs=tuple([vmem] * 4),
        compiler_params=pltpu.CompilerParams(vmem_limit_bytes=16 << 20),
    )(gx, gstep, gcols, few, sums, stretches)


def reduce_kernel(
    hid_ref, cols_ref, few_ref, out_ref, total_ref,
    hid, prod, mate_out, mate_in, a_out, a_own, a_in, a2_out, a2_own, a2_in,
    b_out, b_own, b_in, b2_out, b2_own, b2_in, few, few_c, few_z, few_x, load_sem, ss, rs,
):
    x, z, c, head = place()
    load = pltpu.make_async_copy(hid_ref, hid, load_sem)
    load.start()
    greet(plane_partners(x, z, c, head))
    mate = at(x, z, 1 - c, head)
    started = []

    def send(source, target, k, partner):
        copy = pltpu.make_async_remote_copy(
            source, target, ss.at[k], rs.at[k], device_id=partner, device_id_type=MESH
        )
        copy.start()
        started.append(copy)
        return copy

    few[0] = few_ref[...]
    few_copy = send(few.at[0], few_c, 0, mate)
    load.wait()
    grads = cols_ref[...]
    span = MODEL // NX
    order = (2, 1, 3, 0)
    mate_copies = {}
    for dx in order:
        to = (x + dx) % NX
        chunk = hid[:, pl.ds(pl.multiple_of(to * span, span), span)]
        prod[dx] = dot(chunk, grads, ((0,), (0,))).reshape(NZ, NC, DEPTH, COLS)
        mate_out[dx] = prod[dx, :, 1 - c].astype(BF16)
        mate_copies[dx] = send(mate_out.at[dx], mate_in.at[dx], 1 + dx, mate)
    few_copy.wait_recv()
    few[1] = few[0] + few_c[...]
    few_copies = [
        send(few.at[1], few_z.at[dz - 1], 4 + dz, at(x, z + dz, c, head)) for dz in range(1, NZ)
    ]
    a_copies = []
    for dx in order:
        mate_copies[dx].wait_recv()
        chip = prod[dx, :, c] + mate_in[dx].astype(F32)
        b_own[dx] = chip[:, PART:]
        b_out[:, dx] = chip[:, PART:].astype(BF16)
        if dx:
            a_out[dx - 1] = chip[:, :PART].astype(BF16)
            a_copies.append(send(a_out.at[dx - 1], a_in.at[dx - 1], 11 + dx, at(x + dx, z, c, head)))
        else:
            a_own[...] = chip[:, :PART]
    b_copies = [
        send(b_out.at[(z + dz) % NZ], b_in.at[dz - 1], 14 + dz, at(x, z + dz, c, head))
        for dz in (4, 3, 5, 2, 6, 1, 7)
    ]
    for copy in few_copies:
        copy.wait_recv()
    few[2] = few[1] + jnp.sum(few_z[...], axis=0)
    few_copies = [
        send(few.at[2], few_x.at[dx - 1], 21 + dx, at(x + dx, z, c, head)) for dx in range(1, NX)
    ]
    for copy in b_copies:
        copy.wait_recv()
    b2_own[...] = b_own[:, z] + jnp.sum(b_in[...].astype(F32), axis=0)
    b2_out[...] = b2_own[...].astype(BF16)
    b2_copies = [
        send(b2_out.at[dx], b2_in.at[dx - 1], 24 + dx, at(x + dx, z, c, head)) for dx in range(1, NX)
    ]
    for copy in a_copies:
        copy.wait_recv()
    a2_own[...] = a_own[...] + jnp.sum(a_in[...].astype(F32), axis=0)
    a2_out[...] = a2_own[...].astype(BF16)
    a2_copies = [
        send(a2_out.at[(z + dz) % NZ], a2_in.at[dz - 1], 27 + dz, at(x, z + dz, c, head))
        for dz in (4, 3, 5, 2, 6, 1, 7)
    ]
    for copy in few_copies + b2_copies:
        copy.wait_recv()
    total_ref[...] = few[2] + jnp.sum(few_x[...], axis=0)
    out_ref[PART:] = b2_own[0] + jnp.sum(b2_in[...].astype(F32), axis=0)
    for copy in a2_copies:
        copy.wait_recv()
    out_ref[:PART] = a2_own[z] + jnp.sum(a2_in[...].astype(F32), axis=0)
    for copy in started:
        copy.wait_send()


def reduce_part(hidden, grad_cols, few):
    vmem = pl.BlockSpec(memory_space=pltpu.VMEM)
    shape = jax.ShapeDtypeStruct
    rest = DEPTH - PART
    return pl.pallas_call(
        reduce_kernel,
        name="reduce_part",
        out_shape=(shape((DEPTH, COLS), F32), shape((8, 128), F32)),
        in_specs=[pl.BlockSpec(memory_space=pl.ANY), vmem, vmem],
        out_specs=(vmem, vmem),
        scratch_shapes=[
            pltpu.VMEM((TOK, MODEL), BF16),
            pltpu.VMEM((NX, NZ, NC, DEPTH, COLS), F32),
            pltpu.VMEM((NX, NZ, DEPTH, COLS), BF16),
            pltpu.VMEM((NX, NZ, DEPTH, COLS), BF16),
            pltpu.VMEM((NX - 1, NZ, PART, COLS), BF16),
            pltpu.VMEM((NZ, PART, COLS), F32),
            pltpu.VMEM((NX - 1, NZ, PART, COLS), BF16),
            pltpu.VMEM((NZ, PART, COLS), BF16),
            pltpu.VMEM((NZ, PART, COLS), F32),
            pltpu.VMEM((NZ - 1, PART, COLS), BF16),
            pltpu.VMEM((NZ, NX, rest, COLS), BF16),
            pltpu.VMEM((NX, NZ, rest, COLS), F32),
            pltpu.VMEM((NZ - 1, NX, rest, COLS), BF16),
            pltpu.VMEM((NX, rest, COLS), BF16),
            pltpu.VMEM((NX, rest, COLS), F32),
            pltpu.VMEM((NX - 1, rest, COLS), BF16),
            pltpu.VMEM((3, 8, 128), F32),
            pltpu.VMEM((8, 128), F32),
            pltpu.VMEM((NZ - 1, 8, 128), F32),
            pltpu.VMEM((NX - 1, 8, 128), F32),
            pltpu.SemaphoreType.DMA,
            pltpu.SemaphoreType.DMA((35,)),
            pltpu.SemaphoreType.DMA((35,)),
        ],
        compiler_params=pltpu.CompilerParams(
            collective_id=2, has_side_effects=True, vmem_limit_bytes=VMEM_LIMIT
        ),
    )(hidden, grad_cols, few)


def body(
    hidden, w_bc, x_act, step_size, decay_rate, skip_gain, logp_dir, base_logp, seq_stretches, resp_mask
):
    gx, gstep, gcols, few, sums = front(
        hidden, w_bc, x_act, logp_dir, step_size, decay_rate, skip_gain,
        resp_mask.reshape(1, TOK), base_logp.reshape(1, TOK), seq_stretches,
    )
    grad_x, grad_step, grad_cols, few = finish(gx, gstep, gcols, few, sums, seq_stretches)
    grad_w, total = reduce_part(hidden, grad_cols, few)
    return grad_x, grad_step, total[0, :HEADS], total[1, :HEADS], grad_w


def solution(mesh):
    return jax.shard_map(
        body,
        mesh=mesh,
        in_specs=(
            P("ctx", None),
            P("ctx", "head"),
            P("ctx", "head"),
            P("head", "ctx"),
            P("head"),
            P("head"),
            P("ctx", "head"),
            P("ctx"),
            P(),
            P("ctx"),
        ),
        out_specs=(P("ctx", "head"), P("head", "ctx"), P("head"), P("head"), P("ctx", "head")),
        check_vma=False,
    )
```

time: 108 us -> 93 us (0.86)
  Pallas kernels: 102 us -> 82.5 us
  local copies, waits for them, and re-layouts: 4.91 us -> 9.41 us
    pallas_call x4 -> x2, Pallas kernels: 77.4 us -> 56.9 us  [the longest x1 55.4 us: front(): pl.pallas_call(front_kernel, name='front', out_shape=(shape((TOK, WIDE),...]
    unnamed x27 -> x21, local copies, waits for them, and re-layouts: 4.39 us -> 8.89 us
    pallas_call x1, Pallas kernels: 24.4 us -> 25.7 us  [reduce_part(): pl.pallas_call(reduce_kernel, name='reduce_part', out_shape=(shape((DEPTH...]
where the time goes in v2:
time: 93 us; the launch traced here: 92.6 us
  Pallas kernels  82.5 us (89%)
  local copies, waits for them, and re-layouts  9.41 us (10%)
    pallas_call x1, Pallas kernels, front(): pl.pallas_call(front_kernel, name='front', out_shape=(shape((TOK, WIDE),...  55.4 us
    pallas_call x1, Pallas kernels, reduce_part(): pl.pallas_call(reduce_kernel, name='reduce_part', out_shape=(shape((DEPTH...  25.7 us
    unnamed x21, local copies, waits for them, and re-layouts  8.89 us

profile of v2, /device:TPU:1, one launch (start us, length us, event | category | flops | bytes accessed | tf_op | source)
XLA Modules:
  0.0 92.6 jit_solution(4834756257252925420)
XLA Ops:
  0.6 0.0 copy-start
  0.6 1.6 %copy-done = bf16[256,4096]{1,0:T(8,128)(2,1)S(1)} copy-done((bf16[256,4096]{1,0:T(8,128)(2,1)S(1)}, bf16[256,4096]{1,0:T(8,128)(2,1)}, u32[]{:S(2)}) %copy-start) | copy-done | bytes 2097176
  2.2 0.0 copy-start.1
  2.2 0.9 %copy-done.1 = bf16[256,512]{1,0:T(8,128)(2,1)S(1)} copy-done((bf16[256,512]{1,0:T(8,128)(2,1)S(1)}, bf16[256,512]{1,0:T(8,128)(2,1)}, u32[]{:S(2)}) %copy-start.1) | copy-done | bytes 262168
  3.2 0.0 copy-start.2
  3.2 0.9 %copy-done.2 = bf16[256,512]{1,0:T(8,128)(2,1)S(1)} copy-done((bf16[256,512]{1,0:T(8,128)(2,1)S(1)}, bf16[256,512]{1,0:T(8,128)(2,1)}, u32[]{:S(2)}) %copy-start.2) | copy-done | bytes 262168
  4.1 0.0 copy-start.3
  4.1 0.8 copy-done.3
  4.9 0.0 copy-start.4
  4.9 0.7 copy-done.4
  5.6 0.0 copy-start.5
  5.6 0.7 copy-done.5
  6.2 0.0 copy-start.6
  6.2 0.7 copy-done.6
  6.9 0.0 copy-start.7
  6.9 0.7 copy-done.7
  7.6 0.7 copy-done.8
  8.3 0.0 copy-start.9
  8.3 0.7 copy-done.9
  8.9 55.4 %front.1 = (f32[256,512]{1,0:T(8,128)S(1)}, f32[8,256]{1,0:T(8,128)S(1)}, f32[256,256]{1,0:T(8,128)S(1)}, f32[8,128]{1,0:T(8,128)S(1)}, f32[8,128]{1,0:T(8,128)S(1)}) custom-call(bf16[256,4096]{1,0:T(8,128)(2,1)S(1)} %copy-done, bf16[64,256]{1,0:T(8,128)(2,1)S(1)} %copy-done.3, bf16[256,512]{1,0:T(8,128)(2,1)S(1)} %copy-done.1, ...), custom_call_target="tpu_custom_call" | custom-call | tf_op jit(solution)/shard_map/front/pallas_call | solution.py:550
  64.4 1.4 %finish.1 = (bf16[256,512]{1,0:T(8,128)(2,1)}, f32[8,256]{1,0:T(8,128)}, bf16[256,256]{1,0:T(8,128)(2,1)S(1)}, f32[8,128]{1,0:T(8,128)S(1)}) custom-call(f32[256,512]{1,0:T(8,128)S(1)} %get-tuple-element.16.gx_ref, f32[8,256]{1,0:T(8,128)S(1)} %get-tuple-element.17.gstep_ref, f32[256,256]{1,0:T(8,128)S(1)} %get-tuple-element.18.gcols_ref, ...), custom_call_target="tpu_custom_call" | custom-call | tf_op jit(solution)/shard_map/finish/pallas_call | solution.py:628
  65.8 25.7 %reduce_part.1 = (f32[64,256]{1,0:T(8,128)S(1)}, f32[8,128]{1,0:T(8,128)S(1)}) custom-call(bf16[256,4096]{1,0:T(8,128)(2,1)S(1)} %copy-done, bf16[256,256]{1,0:T(8,128)(2,1)S(1)} %get-tuple-element.23.cols_ref, f32[8,128]{1,0:T(8,128)S(1)} %get-tuple-element.24.few_ref), custom_call_target="tpu_custom_call" | custom-call | tf_op jit(solution)/shard_map/reduce_part/pallas_call | solution.py:732
  91.4 0.5 slice_bitcast_fusion
  92.0 0.6 copy.16
  (1 shorter events, 0.0 us)
Async XLA Ops:
  0.6 1.6 %copy-start = (bf16[256,4096]{1,0:T(8,128)(2,1)S(1)}, bf16[256,4096]{1,0:T(8,128)(2,1)}, u32[]{:S(2)}) copy-start(bf16[256,4096]{1,0:T(8,128)(2,1)} %hid_ref.1) | copy-start | bytes 6291460
  2.2 0.9 %copy-start.1 = (bf16[256,512]{1,0:T(8,128)(2,1)S(1)}, bf16[256,512]{1,0:T(8,128)(2,1)}, u32[]{:S(2)}) copy-start(bf16[256,512]{1,0:T(8,128)(2,1)} %x_hbm.1) | copy-start | bytes 786436
  3.2 0.9 %copy-start.2 = (bf16[256,512]{1,0:T(8,128)(2,1)S(1)}, bf16[256,512]{1,0:T(8,128)(2,1)}, u32[]{:S(2)}) copy-start(bf16[256,512]{1,0:T(8,128)(2,1)} %dir_hbm.1) | copy-start | bytes 786436
  4.1 0.8 copy-start.3
  4.9 0.7 copy-start.4
  5.6 0.7 copy-start.5
  6.2 0.7 copy-start.6
  6.9 0.7 copy-start.7
  7.6 0.7 copy-start.8
  8.3 0.7 copy-start.9

commit v3 on v2

--- a/solution.py
+++ b/solution.py
@@ -20,14 +20,20 @@
 COLS = 2 * NSTATE
 MODEL = NCTX * DEPTH
 PART = 48
+AHEAD = 3
 
 hinge_sharp = 0.005
 hinge_margin = 10.0
+
+FAR_FIRST = sorted(
+    [(dx, dz) for dx in range(NX) for dz in range(NZ) if dx or dz],
+    key=lambda step: -(min(step[0], NX - step[0]) + min(step[1], NZ - step[1])),
+)
 
 MESH = pl.DeviceIdType.MESH
 F32 = jnp.float32
 BF16 = jnp.bfloat16
-VMEM_LIMIT = 48 << 20
+VMEM_LIMIT = 64 << 20
 SPACE = pltpu.HBM
 
 
@@ -38,21 +44,6 @@
 
 def at(x, z, c, head):
     return (((x % NX) * NZ + (z % NZ)) * NC + c, head)
-
-
-def greet(partners):
-    barrier = pltpu.get_barrier_semaphore()
-    for partner in partners:
-        pl.semaphore_signal(barrier, inc=1, device_id=partner, device_id_type=MESH)
-    pl.semaphore_wait(barrier, len(partners))
-
-
-def plane_partners(x, z, c, head):
-    return (
-        [at(x, z + dz, c, head) for dz in range(1, NZ)]
-        + [at(x + dx, z, c, head) for dx in range(1, NX)]
-        + [at(x, z, 1 - c, head)]
-    )
 
 
 def dot(left, right, dims=((1,), (0,)), precision=None):
@@ -86,12 +77,15 @@
     return sum((block >= start).astype(jnp.int32) for start in starts)
 
 
-def front_kernel(
+def whole_kernel(
     hid_hbm, w_hbm, x_hbm, dir_hbm, step_hbm, rate_hbm, skip_hbm, mask_hbm, base_hbm, stretch_hbm,
-    gx_ref, gstep_ref, gcols_ref, few_ref, sums_ref,
+    grad_x_out, grad_step_out, rate_out, skip_out, grad_w_out,
     hid, x_ref, dir_ref, step_ref, rate_ref, skip_ref, mask_ref, base_ref, stretch_ref,
     buf, dec, factors, moves, stack, cols_ref, xf_ref, dyg_ref, drow, dcol, lg, mate_lg, msg, got, wide,
     swept, reply, states, tab, part, near, across,
+    gx_ref, gcols_ref, gx_bf, gstep_ref, gw_ref, small,
+    prod, mate_out, mate_in, a_out, a_own, a_in, a2_out, a2_in, b_out, bz_in, b2_out, b2_in,
+    few, few_c, few_z, few_x,
     load_sem, send_sem, recv_sem, ss, rs, gs, gr,
 ):
     index = lax.axis_index("ctx")
@@ -100,6 +94,16 @@
     mate = at(x, z, 1 - c, head)
     every = slice(None)
 
+    barrier = pltpu.get_barrier_semaphore()
+
+    def hello(partner):
+        pl.semaphore_signal(barrier, inc=1, device_id=partner, device_id_type=MESH)
+
+    for dz in (4, 3, 5, 2, 6, 1, 7):
+        hello(at(x, z + dz, c, head))
+    for dx in (2, 1, 3):
+        hello(at(x + dx, z, c, head))
+    hello(mate)
     loads = {}
     for k, (name, source, target) in enumerate(
         (
@@ -118,23 +122,10 @@
         loads[name] = pltpu.make_async_copy(source, target, load_sem.at[k])
         loads[name].start()
 
-    barrier = pltpu.get_barrier_semaphore()
-
-    def hello(k, carry):
-        to = (chip + k) % CHIPS
-        pl.semaphore_signal(barrier, inc=1, device_id=(to * 2 + c, head), device_id_type=MESH)
-        return carry
-
-    def hello_head(k, carry):
-        to = (head + k // 2) % NHEAD
-        who = chip * 2 + (c + k) % 2
-        pl.semaphore_signal(barrier, inc=1, device_id=(who, to), device_id_type=MESH)
-        return carry
-
-    lax.fori_loop(1, CHIPS, hello, 0)
-    lax.fori_loop(1, 2 * NHEAD, hello_head, 0)
+    for k in range(2, 2 * NHEAD):
+        hello((chip * 2 + (c + k) % 2, (head + k // 2) % NHEAD))
     loads["w"].wait()
-    pl.semaphore_wait(barrier, CHIPS - 1 + 2 * NHEAD - 1)
+    pl.semaphore_wait(barrier, NZ - 1 + NX - 1 + 2 * NHEAD - 1)
 
     started, slots = [], {}
 
@@ -150,6 +141,14 @@
             rs.at[k],
             device_id=partner,
             device_id_type=MESH,
+        )
+        copy.start()
+        started.append(copy)
+
+    def send_few(source, target, into, key, partner):
+        k = slot(key)
+        copy = pltpu.make_async_remote_copy(
+            few.at[source], target.at[into], ss.at[k], rs.at[k], device_id=partner, device_id_type=MESH
         )
         copy.start()
         started.append(copy)
@@ -359,8 +358,8 @@
     ).astype(BF16)
 
     def exchange(source, target, phase):
-        def start(k, carry):
-            to = (chip + k) % CHIPS
+        for dx, dz in FAR_FIRST:
+            to = ((x + dx) % NX) * NZ + (z + dz) % NZ
             pltpu.make_async_remote_copy(
                 source.at[to],
                 target.at[chip],
@@ -369,9 +368,6 @@
                 device_id=(to * 2 + c, head),
                 device_id_type=MESH,
             ).start()
-            return carry
-
-        lax.fori_loop(1, CHIPS, start, 0)
 
     def settle(target, sem):
         rest = target.at[pl.ds(0, CHIPS - 1)]
@@ -405,7 +401,6 @@
     wide_lane = lax.broadcasted_iota(jnp.int32, (WIDE, 128), 1)
     overlap_row = jnp.broadcast_to(jnp.concatenate(overlap, axis=1), (8, WIDE))
     overlap_head = dot(overlap_row, (wide_row == wide_lane).astype(F32), precision=lax.Precision.HIGHEST)
-    few_ref[...] = overlap_head
     skip_row = jnp.zeros((1, 128), F32)
     for h in range(HEADS):
         skip_row = jnp.where(lane1 == h, skip_ref[h], skip_row)
@@ -444,25 +439,26 @@
 
     zero = jnp.zeros((8, 128), F32)
     lax.fori_loop(0, CHIPS, advance, (zero, zero))
-    reply[...] = swept[...].astype(BF16)
-    exchange(reply, states.at[c], 1)
-    states[c, chip] = reply[chip]
-
     met = jnp.sum(swept[:, 0:8] * wide[:, 8:16], axis=1) * enters
     met = jnp.sum(met, axis=1, keepdims=True)
     seqs = seq_of(2 * chips, starts)
     mine = mine + jnp.sum(jnp.where(lane32 == seqs, met, 0.0), axis=0, keepdims=True)
     part[0] = mine
 
-    def spread(k, carry):
-        to = (chip + k) % CHIPS
+    for k, (dx, dz) in enumerate(FAR_FIRST):
+        to = ((x + dx) % NX) * NZ + (z + dz) % NZ
         pltpu.make_async_remote_copy(
-            part.at[0], near.at[k], gs.at[0], gr.at[0], device_id=(to * 2 + c, head), device_id_type=MESH
+            part.at[0],
+            near.at[k + 1],
+            gs.at[0],
+            gr.at[0],
+            device_id=(to * 2 + c, head),
+            device_id_type=MESH,
         ).start()
-        return carry
-
-    lax.fori_loop(1, CHIPS, spread, 0)
     near[0] = mine
+    reply[...] = swept[...].astype(BF16)
+    exchange(reply, states.at[c], 1)
+    states[c, chip] = reply[chip]
 
     def settle_few(target, sem, count):
         rest = target.at[pl.ds(1, count)]
@@ -528,37 +524,145 @@
     token = lax.broadcasted_iota(jnp.int32, (8, TOK), 1)
     grad_cum = drow[...] - dcol[...] + carried - kept + jnp.where(token == TOK - 1, end, 0.0)
     tail = dot(grad_cum, (s_index >= t_index).astype(F32), precision=lax.Precision.HIGHEST)
-    gstep_ref[...] = (dcol[...] + kept) / step - rate * tail
+    grad_step = (dcol[...] + kept) / step - rate * tail
     grad_rate = -jnp.sum(step * tail, axis=1, keepdims=True)
     rate_row = jnp.sum(jnp.where(lanes8 == rows8, grad_rate, 0.0), axis=0, keepdims=True)
-    few_ref[...] = jnp.where(rows8 == 0, rate_row, few_ref[...])
-
+
+    grads = gcols_ref[...].astype(BF16)
+    order = (4, 3, 5, 2, 6, 1, 7, 0)
+
+    def multiply(k):
+        zz = (z + order[k]) % NZ
+        for dx in range(NX):
+            first_column = (((x + dx) % NX) * NZ + zz) * (NC * DEPTH)
+            chunk = hid[:, pl.ds(pl.multiple_of(first_column, NC * DEPTH), NC * DEPTH)]
+            prod[k, dx] = dot(chunk, grads, ((0,), (0,))).reshape(NC, DEPTH, COLS)
+            mate_out[k, dx] = prod[k, dx, other].astype(BF16)
+        send(mate_out, (k,), ("m", k), mate, mate_in)
+
+    def scale_of(block, seq_sums):
+        one, two, three = starts
+        chosen = jnp.where(block >= two, 2, 0)
+        signed = jnp.where(lane1 == chosen, seq_sums, 0.0) - jnp.where(lane1 == chosen + 1, seq_sums, 0.0)
+        margin = jnp.sum(signed, axis=1, keepdims=True)
+        coef = 1.0 / (1.0 + jnp.exp(-hinge_sharp * (hinge_margin - margin)))
+        rejected = ((block >= one) & (block < two)) | (block >= three)
+        return jnp.where(rejected, coef, -coef)
+
+    def combine(k):
+        dz = order[k]
+        arrive(mate_in, (k,), ("m", k))
+        for dx in (2, 1, 3):
+            both = prod[k, dx, c] * scale + mate_in[k, dx].astype(F32) * scale_mate
+            a_out[k, dx - 1] = both[:PART].astype(BF16)
+            send(a_out, (k, dx - 1), ("a", k, dx), to_x(dx), a_in)
+            prod[k, dx, c, PART:] = both[PART:]
+        both = prod[k, 0, c] * scale + mate_in[k, 0].astype(F32) * scale_mate
+        a_own[k] = both[:PART]
+        prod[k, 0, c, PART:] = both[PART:]
+        if dz:
+            b_out[k] = prod[k, :, c, PART:].astype(BF16)
+            send(b_out, (k,), ("b", k), to_z(dz), bz_in)
+
+    def pass_on(k):
+        dz = order[k]
+        for dx in (1, 2, 3):
+            arrive(a_in, (k, dx - 1), ("a", k, dx))
+        a_own[k] = a_own[k] + jnp.sum(a_in[k].astype(F32), axis=0)
+        if dz:
+            a2_out[k] = a_own[k].astype(BF16)
+            send(a2_out, (k,), ("a2", k), to_z(dz), a2_in)
+
+    for k in range(AHEAD):
+        multiply(k)
     settle_few(across, gr.at[1], 2 * NHEAD - 1)
-    sums_ref[...] = jnp.broadcast_to(jnp.sum(across[...], axis=0), (8, 128))
+    seq_sums = jnp.sum(across[...], axis=0)
+    scale, scale_mate = scale_of(index, seq_sums), scale_of(index + 1 - 2 * c, seq_sums)
+    for k in range(NZ):
+        combine(k)
+        if k + AHEAD < NZ:
+            multiply(k + AHEAD)
+
+    few[0] = jnp.where(rows8 == 0, rate_row, overlap_head) * scale
+    send(few, (0,), ("fc",), mate, few_c)
+    gx_bf[...] = (gx_ref[...] * scale).astype(BF16)
+    gstep_ref[...] = grad_step * scale
+    stores = [
+        pltpu.make_async_copy(gx_bf, grad_x_out, load_sem.at[0]),
+        pltpu.make_async_copy(gstep_ref, grad_step_out, load_sem.at[1]),
+    ]
+    for store in stores:
+        store.start()
+    arrive(few_c, (0,), ("fc",))
+    few[1] = few[0] + few_c[0]
+
+    pass_on(0)
+    for dz in near_z:
+        send_few(1, few_z, dz - 1, ("fz", dz), to_z(dz))
+    for k in range(1, 4):
+        pass_on(k)
+    for dz in near_z:
+        arrive(few_z, (dz - 1,), ("fz", dz))
+    few[2] = few[1] + jnp.sum(few_z[...], axis=0)
+    for dx in near_x:
+        send_few(2, few_x, dx - 1, ("fx", dx), to_x(dx))
+    pass_on(4)
+    b_sum = prod[NZ - 1, :, c, PART:]
+    for k in range(NZ - 1):
+        arrive(bz_in, (k,), ("b", k))
+        b_sum = b_sum + bz_in[k].astype(F32)
+    for dx in (2, 1, 3):
+        b2_out[dx - 1] = b_sum[dx].astype(BF16)
+        send(b2_out, (dx - 1,), ("b2", dx), to_x(dx), b2_in)
+    for k in range(5, NZ):
+        pass_on(k)
+    for dx in near_x:
+        arrive(few_x, (dx - 1,), ("fx", dx))
+    small[...] = few[2] + jnp.sum(few_x[...], axis=0)
+    for h in range(HEADS):
+        rate_ref[h] = small[0, h]
+        skip_ref[h] = small[1, h]
+    stores.append(pltpu.make_async_copy(rate_ref, rate_out, load_sem.at[2]))
+    stores.append(pltpu.make_async_copy(skip_ref, skip_out, load_sem.at[4]))
+    stores[-2].start()
+    stores[-1].start()
+    for dx in near_x:
+        arrive(b2_in, (dx - 1,), ("b2", dx))
+    gw_ref[PART:] = b_sum[0] + jnp.sum(b2_in[...].astype(F32), axis=0)
+    a_sum = a_own[NZ - 1]
+    for k in range(NZ - 1):
+        arrive(a2_in, (k,), ("a2", k))
+        a_sum = a_sum + a2_in[k].astype(F32)
+    gw_ref[:PART] = a_sum
+    stores.append(pltpu.make_async_copy(gw_ref, grad_w_out, load_sem.at[3]))
+    stores[-1].start()
+
     for copy in started:
         copy.wait_send()
     settle(msg, send_sem.at[0])
     settle(reply, send_sem.at[1])
     settle_few(near, gs.at[0], CHIPS - 1)
     settle_few(across, gs.at[1], 2 * NHEAD - 1)
-
-
-def front(hidden, w_bc, x_act, logp_dir, step_size, rate, skip, mask, base, stretches):
+    for store in stores:
+        store.wait()
+
+
+def whole(hidden, w_bc, x_act, logp_dir, step_size, rate, skip, mask, base, stretches):
     shape = jax.ShapeDtypeStruct
-    vmem = pl.BlockSpec(memory_space=pltpu.VMEM)
-    count = 120
+    rest = DEPTH - PART
+    count = 190
     return pl.pallas_call(
-        front_kernel,
-        name="front",
+        whole_kernel,
+        name="whole",
         out_shape=(
-            shape((TOK, WIDE), F32),
+            shape((TOK, WIDE), BF16),
             shape((8, TOK), F32),
-            shape((TOK, COLS), F32),
-            shape((8, 128), F32),
-            shape((8, 128), F32),
+            shape((HEADS,), F32),
+            shape((HEADS,), F32),
+            shape((DEPTH, COLS), F32),
         ),
         in_specs=[pl.BlockSpec(memory_space=SPACE)] * 10,
-        out_specs=tuple([vmem] * 5),
+        out_specs=tuple([pl.BlockSpec(memory_space=SPACE)] * 5),
         scratch_shapes=[
             pltpu.VMEM((TOK, MODEL), BF16),
             pltpu.VMEM((TOK, WIDE), BF16),
@@ -591,6 +695,28 @@
             pltpu.VMEM((2, 1, 128), F32),
             pltpu.VMEM((CHIPS, 1, 128), F32),
             pltpu.VMEM((2 * NHEAD, 1, 128), F32),
+            pltpu.VMEM((TOK, WIDE), F32),
+            pltpu.VMEM((TOK, COLS), F32),
+            pltpu.VMEM((TOK, WIDE), BF16),
+            pltpu.VMEM((8, TOK), F32),
+            pltpu.VMEM((DEPTH, COLS), F32),
+            pltpu.VMEM((8, 128), F32),
+            pltpu.VMEM((NZ, NX, NC, DEPTH, COLS), F32),
+            pltpu.VMEM((NZ, NX, DEPTH, COLS), BF16),
+            pltpu.VMEM((NZ, NX, DEPTH, COLS), BF16),
+            pltpu.VMEM((NZ, NX - 1, PART, COLS), BF16),
+            pltpu.VMEM((NZ, PART, COLS), F32),
+            pltpu.VMEM((NZ, NX - 1, PART, COLS), BF16),
+            pltpu.VMEM((NZ - 1, PART, COLS), BF16),
+            pltpu.VMEM((NZ - 1, PART, COLS), BF16),
+            pltpu.VMEM((NZ - 1, NX, rest, COLS), BF16),
+            pltpu.VMEM((NZ - 1, NX, rest, COLS), BF16),
+            pltpu.VMEM((NX - 1, rest, COLS), BF16),
+            pltpu.VMEM((NX - 1, rest, COLS), BF16),
+            pltpu.VMEM((3, 8, 128), F32),
+            pltpu.VMEM((1, 8, 128), F32),
+            pltpu.VMEM((NZ - 1, 8, 128), F32),
+            pltpu.VMEM((NX - 1, 8, 128), F32),
             pltpu.SemaphoreType.DMA((10,)),
             pltpu.SemaphoreType.DMA((2,)),
             pltpu.SemaphoreType.DMA((2,)),
@@ -605,177 +731,46 @@
     )(hidden, w_bc, x_act, logp_dir, step_size, rate, skip, mask, base, stretches)
 
 
-def finish_kernel(gx_ref, gstep_ref, gcols_ref, few_ref, sums_ref, stretch_ref, grad_x_ref, grad_step_ref, cols_ref, small_ref):
-    index = lax.axis_index("ctx")
-    one, two, three = sequence_starts(stretch_ref)
-    sums = sums_ref[0:1]
-    lane = lax.broadcasted_iota(jnp.int32, (1, 128), 1)
-    base = jnp.where(index >= two, 2, 0)
-    signed = jnp.where(lane == base, sums, 0.0) - jnp.where(lane == base + 1, sums, 0.0)
-    margin = jnp.sum(signed, axis=1, keepdims=True)
-    coef = 1.0 / (1.0 + jnp.exp(-hinge_sharp * (hinge_margin - margin)))
-    rejected = ((index >= one) & (index < two)) | (index >= three)
-    scale = jnp.where(rejected, coef, -coef)
-    grad_x_ref[...] = (gx_ref[...] * scale).astype(BF16)
-    grad_step_ref[...] = gstep_ref[...] * scale
-    cols_ref[...] = (gcols_ref[...] * scale).astype(BF16)
-    small_ref[...] = few_ref[...] * scale
-
-
-def finish(gx, gstep, gcols, few, sums, stretches):
-    vmem = pl.BlockSpec(memory_space=pltpu.VMEM)
-    shape = jax.ShapeDtypeStruct
+def finish_kernel(*refs):
+    *ends, sems = refs
+    count = len(ends) // 3
+    sources, targets, holds = ends[:count], ends[count : 2 * count], ends[2 * count :]
+    into = [pltpu.make_async_copy(sources[k], holds[k], sems.at[k]) for k in range(count)]
+    back = [pltpu.make_async_copy(holds[k], targets[k], sems.at[count + k]) for k in range(count)]
+    for copy in into:
+        copy.start()
+    for k in reversed(range(count)):
+        into[k].wait()
+        back[k].start()
+    for copy in back:
+        copy.wait()
+
+
+def finish(*arrays):
+    spec = pl.BlockSpec(memory_space=SPACE)
     return pl.pallas_call(
         finish_kernel,
         name="finish",
-        out_shape=(
-            shape((TOK, WIDE), BF16),
-            shape((8, TOK), F32),
-            shape((TOK, COLS), BF16),
-            shape((8, 128), F32),
-        ),
-        in_specs=[vmem] * 5 + [pl.BlockSpec(memory_space=pltpu.SMEM)],
-        out_specs=tuple([vmem] * 4),
-        compiler_params=pltpu.CompilerParams(vmem_limit_bytes=16 << 20),
-    )(gx, gstep, gcols, few, sums, stretches)
-
-
-def reduce_kernel(
-    hid_ref, cols_ref, few_ref, out_ref, total_ref,
-    hid, prod, mate_out, mate_in, a_out, a_own, a_in, a2_out, a2_own, a2_in,
-    b_out, b_own, b_in, b2_out, b2_own, b2_in, few, few_c, few_z, few_x, load_sem, ss, rs,
-):
-    x, z, c, head = place()
-    load = pltpu.make_async_copy(hid_ref, hid, load_sem)
-    load.start()
-    greet(plane_partners(x, z, c, head))
-    mate = at(x, z, 1 - c, head)
-    started = []
-
-    def send(source, target, k, partner):
-        copy = pltpu.make_async_remote_copy(
-            source, target, ss.at[k], rs.at[k], device_id=partner, device_id_type=MESH
-        )
-        copy.start()
-        started.append(copy)
-        return copy
-
-    few[0] = few_ref[...]
-    few_copy = send(few.at[0], few_c, 0, mate)
-    load.wait()
-    grads = cols_ref[...]
-    span = MODEL // NX
-    order = (2, 1, 3, 0)
-    mate_copies = {}
-    for dx in order:
-        to = (x + dx) % NX
-        chunk = hid[:, pl.ds(pl.multiple_of(to * span, span), span)]
-        prod[dx] = dot(chunk, grads, ((0,), (0,))).reshape(NZ, NC, DEPTH, COLS)
-        mate_out[dx] = prod[dx, :, 1 - c].astype(BF16)
-        mate_copies[dx] = send(mate_out.at[dx], mate_in.at[dx], 1 + dx, mate)
-    few_copy.wait_recv()
-    few[1] = few[0] + few_c[...]
-    few_copies = [
-        send(few.at[1], few_z.at[dz - 1], 4 + dz, at(x, z + dz, c, head)) for dz in range(1, NZ)
-    ]
-    a_copies = []
-    for dx in order:
-        mate_copies[dx].wait_recv()
-        chip = prod[dx, :, c] + mate_in[dx].astype(F32)
-        b_own[dx] = chip[:, PART:]
-        b_out[:, dx] = chip[:, PART:].astype(BF16)
-        if dx:
-            a_out[dx - 1] = chip[:, :PART].astype(BF16)
-            a_copies.append(send(a_out.at[dx - 1], a_in.at[dx - 1], 11 + dx, at(x + dx, z, c, head)))
-        else:
-            a_own[...] = chip[:, :PART]
-    b_copies = [
-        send(b_out.at[(z + dz) % NZ], b_in.at[dz - 1], 14 + dz, at(x, z + dz, c, head))
-        for dz in (4, 3, 5, 2, 6, 1, 7)
-    ]
-    for copy in few_copies:
-        copy.wait_recv()
-    few[2] = few[1] + jnp.sum(few_z[...], axis=0)
-    few_copies = [
-        send(few.at[2], few_x.at[dx - 1], 21 + dx, at(x + dx, z, c, head)) for dx in range(1, NX)
-    ]
-    for copy in b_copies:
-        copy.wait_recv()
-    b2_own[...] = b_own[:, z] + jnp.sum(b_in[...].astype(F32), axis=0)
-    b2_out[...] = b2_own[...].astype(BF16)
-    b2_copies = [
-        send(b2_out.at[dx], b2_in.at[dx - 1], 24 + dx, at(x + dx, z, c, head)) for dx in range(1, NX)
-    ]
-    for copy in a_copies:
-        copy.wait_recv()
-    a2_own[...] = a_own[...] + jnp.sum(a_in[...].astype(F32), axis=0)
-    a2_out[...] = a2_own[...].astype(BF16)
-    a2_copies = [
-        send(a2_out.at[(z + dz) % NZ], a2_in.at[dz - 1], 27 + dz, at(x, z + dz, c, head))
-        for dz in (4, 3, 5, 2, 6, 1, 7)
-    ]
-    for copy in few_copies + b2_copies:
-        copy.wait_recv()
-    total_ref[...] = few[2] + jnp.sum(few_x[...], axis=0)
-    out_ref[PART:] = b2_own[0] + jnp.sum(b2_in[...].astype(F32), axis=0)
-    for copy in a2_copies:
-        copy.wait_recv()
-    out_ref[:PART] = a2_own[z] + jnp.sum(a2_in[...].astype(F32), axis=0)
-    for copy in started:
-        copy.wait_send()
-
-
-def reduce_part(hidden, grad_cols, few):
-    vmem = pl.BlockSpec(memory_space=pltpu.VMEM)
-    shape = jax.ShapeDtypeStruct
-    rest = DEPTH - PART
-    return pl.pallas_call(
-        reduce_kernel,
-        name="reduce_part",
-        out_shape=(shape((DEPTH, COLS), F32), shape((8, 128), F32)),
-        in_specs=[pl.BlockSpec(memory_space=pl.ANY), vmem, vmem],
-        out_specs=(vmem, vmem),
+        out_shape=tuple(jax.ShapeDtypeStruct(array.shape, array.dtype) for array in arrays),
+        in_specs=[spec] * len(arrays),
+        out_specs=tuple([spec] * len(arrays)),
         scratch_shapes=[
-            pltpu.VMEM((TOK, MODEL), BF16),
-            pltpu.VMEM((NX, NZ, NC, DEPTH, COLS), F32),
-            pltpu.VMEM((NX, NZ, DEPTH, COLS), BF16),
-            pltpu.VMEM((NX, NZ, DEPTH, COLS), BF16),
-            pltpu.VMEM((NX - 1, NZ, PART, COLS), BF16),
-            pltpu.VMEM((NZ, PART, COLS), F32),
-            pltpu.VMEM((NX - 1, NZ, PART, COLS), BF16),
-            pltpu.VMEM((NZ, PART, COLS), BF16),
-            pltpu.VMEM((NZ, PART, COLS), F32),
-            pltpu.VMEM((NZ - 1, PART, COLS), BF16),
-            pltpu.VMEM((NZ, NX, rest, COLS), BF16),
-            pltpu.VMEM((NX, NZ, rest, COLS), F32),
-            pltpu.VMEM((NZ - 1, NX, rest, COLS), BF16),
-            pltpu.VMEM((NX, rest, COLS), BF16),
-            pltpu.VMEM((NX, rest, COLS), F32),
-            pltpu.VMEM((NX - 1, rest, COLS), BF16),
-            pltpu.VMEM((3, 8, 128), F32),
-            pltpu.VMEM((8, 128), F32),
-            pltpu.VMEM((NZ - 1, 8, 128), F32),
-            pltpu.VMEM((NX - 1, 8, 128), F32),
-            pltpu.SemaphoreType.DMA,
-            pltpu.SemaphoreType.DMA((35,)),
-            pltpu.SemaphoreType.DMA((35,)),
-        ],
-        compiler_params=pltpu.CompilerParams(
-            collective_id=2, has_side_effects=True, vmem_limit_bytes=VMEM_LIMIT
-        ),
-    )(hidden, grad_cols, few)
+            (pltpu.VMEM if array.ndim == 2 else pltpu.SMEM)(array.shape, array.dtype) for array in arrays
+        ]
+        + [pltpu.SemaphoreType.DMA((2 * len(arrays),))],
+        compiler_params=pltpu.CompilerParams(vmem_limit_bytes=VMEM_LIMIT),
+    )(*arrays)
 
 
 def body(
     hidden, w_bc, x_act, step_size, decay_rate, skip_gain, logp_dir, base_logp, seq_stretches, resp_mask
 ):
-    gx, gstep, gcols, few, sums = front(
-        hidden, w_bc, x_act, logp_dir, step_size, decay_rate, skip_gain,
-        resp_mask.reshape(1, TOK), base_logp.reshape(1, TOK), seq_stretches,
+    return finish(
+        *whole(
+            hidden, w_bc, x_act, logp_dir, step_size, decay_rate, skip_gain,
+            resp_mask.reshape(1, TOK), base_logp.reshape(1, TOK), seq_stretches,
+        )
     )
-    grad_x, grad_step, grad_cols, few = finish(gx, gstep, gcols, few, sums, seq_stretches)
-    grad_w, total = reduce_part(hidden, grad_cols, few)
-    return grad_x, grad_step, total[0, :HEADS], total[1, :HEADS], grad_w
 
 
 def solution(mesh):

time: 93 us -> 71.4 us (0.77)
  Pallas kernels: 82.5 us -> 70.1 us
  local copies, waits for them, and re-layouts: 9.41 us -> 0 us
    pallas_call x3 -> x2, Pallas kernels: 82.5 us -> 70.1 us  [the longest x1 68.3 us: whole(): pl.pallas_call(whole_kernel, name='whole', out_shape=(shape((TOK, WIDE),...]
    unnamed x21 -> x0, local copies, waits for them, and re-layouts: 8.89 us -> none
where the time goes in v3:
time: 71.4 us; the launch traced here: 70.7 us
  Pallas kernels  70.1 us (98%)
    pallas_call x1, Pallas kernels, whole(): pl.pallas_call(whole_kernel, name='whole', out_shape=(shape((TOK, WIDE),...  68.3 us
    pallas_call x1, Pallas kernels, finish(): pl.pallas_call(finish_kernel, name='finish', out_shape=tuple((jax.ShapeDt...  1.77 us

profile of v3, /device:TPU:1, one launch (start us, length us, event | category | flops | bytes accessed | tf_op | source)
XLA Modules:
  0.0 70.7 jit_solution(1266324918674959799)
XLA Ops:
  0.6 68.3 %whole.1 = (bf16[256,512]{1,0:T(8,128)(2,1)}, f32[8,256]{1,0:T(8,128)}, f32[8]{0:T(128)}, f32[8]{0:T(128)}, f32[64,256]{1,0:T(8,128)}) custom-call(bf16[256,4096]{1,0:T(8,128)(2,1)} %hid_hbm.1, bf16[64,256]{1,0:T(8,128)(2,1)} %w_hbm.1, bf16[256,512]{1,0:T(8,128)(2,1)} %x_hbm.1, bf16[256,512]{1,0:T(8,128)(2,1)} %dir_hbm.1, f32[8,256]{1,0:T(8,128)} %step_hbm.1, ...), custom_call_target="tpu_custom_call" | custom-call | tf_op jit(solution)/shard_map/whole/pallas_call | solution.py:654
  69.0 1.8 %finish.1 = (bf16[256,512]{1,0:T(8,128)(2,1)}, f32[8,256]{1,0:T(8,128)}, f32[8]{0:T(128)}, f32[8]{0:T(128)}, f32[64,256]{1,0:T(8,128)}) custom-call(bf16[256,512]{1,0:T(8,128)(2,1)} %get-tuple-element.10.refs_0_, f32[8,256]{1,0:T(8,128)} %get-tuple-element.11.refs_1_, f32[8]{0:T(128)} %get-tuple-element.12.refs_2_, f32[8]{0:T(128)} %get-tuple-element.13.refs_3_, ...), custom_call_target="tpu_custom_call" | custom-call | tf_op jit(solution)/shard_map/finish/pallas_call | solution.py:751

commit v4 on v3

--- a/solution.py
+++ b/solution.py
@@ -20,7 +20,7 @@
 COLS = 2 * NSTATE
 MODEL = NCTX * DEPTH
 PART = 48
-AHEAD = 3
+AHEAD = 4
 
 hinge_sharp = 0.005
 hinge_margin = 10.0
@@ -29,6 +29,8 @@
     [(dx, dz) for dx in range(NX) for dz in range(NZ) if dx or dz],
     key=lambda step: -(min(step[0], NX - step[0]) + min(step[1], NZ - step[1])),
 )
+
+HEADS_FAR_FIRST = (8, 9, 6, 7, 10, 11, 4, 5, 12, 13, 2, 3, 14, 15, 1)
 
 MESH = pl.DeviceIdType.MESH
 F32 = jnp.float32
@@ -83,9 +85,9 @@
     hid, x_ref, dir_ref, step_ref, rate_ref, skip_ref, mask_ref, base_ref, stretch_ref,
     buf, dec, factors, moves, stack, cols_ref, xf_ref, dyg_ref, drow, dcol, lg, mate_lg, msg, got, wide,
     swept, reply, states, tab, part, near, across,
-    gx_ref, gcols_ref, gx_bf, gstep_ref, gw_ref, small,
+    hid_t, xf_t, dyg_t, gx_ref, gcols_ref, gx_bf, gstep_ref, gw_ref,
     prod, mate_out, mate_in, a_out, a_own, a_in, a2_out, a2_in, b_out, bz_in, b2_out, b2_in,
-    few, few_c, few_z, few_x,
+    few, few_c, few_all,
     load_sem, send_sem, recv_sem, ss, rs, gs, gr,
 ):
     index = lax.axis_index("ctx")
@@ -127,41 +129,34 @@
     loads["w"].wait()
     pl.semaphore_wait(barrier, NZ - 1 + NX - 1 + 2 * NHEAD - 1)
 
-    started, slots = [], {}
-
-    def slot(key):
-        return slots.setdefault(key, len(slots))
-
-    def send(ref, where, key, partner, into=None):
-        k = slot(key)
-        copy = pltpu.make_async_remote_copy(
-            ref.at[where],
-            (ref if into is None else into).at[where],
-            ss.at[k],
-            rs.at[k],
+    sent, landed = {}, {}
+
+    def slot(table, key):
+        return table.setdefault(key, len(table))
+
+    def move(source, target, out, key, partner):
+        pltpu.make_async_remote_copy(
+            source,
+            target,
+            ss.at[slot(sent, out)],
+            rs.at[slot(landed, key)],
             device_id=partner,
             device_id_type=MESH,
-        )
-        copy.start()
-        started.append(copy)
-
-    def send_few(source, target, into, key, partner):
-        k = slot(key)
-        copy = pltpu.make_async_remote_copy(
-            few.at[source], target.at[into], ss.at[k], rs.at[k], device_id=partner, device_id_type=MESH
-        )
-        copy.start()
-        started.append(copy)
+        ).start()
+
+    def send(ref, where, out, key, partner, into=None):
+        move(ref.at[where], (ref if into is None else into).at[where], out, key, partner)
 
     def arrive(ref, where, key):
         piece = ref.at[where]
-        k = slot(key)
-        pltpu.make_async_remote_copy(
-            piece, piece, ss.at[k], rs.at[k], device_id=mate, device_id_type=MESH
-        ).wait_recv()
+        pltpu.make_async_copy(piece, piece, rs.at[slot(landed, key)]).wait()
+
+    def drain(out, piece):
+        pltpu.make_async_copy(piece, piece, ss.at[sent.pop(out)]).wait()
 
     low, high = pl.ds(0, PART), pl.ds(PART, DEPTH - PART)
     near_z, near_x = (1, 7, 2, 6, 3, 5, 4), (1, 3, 2)
+    far_z, far_x = (4, 3, 5, 2, 6, 1, 7), (2, 1, 3)
 
     def to_z(dz):
         return at(x, z + dz, c, head)
@@ -176,14 +171,14 @@
         return (x - dx) % NX
 
     for dz in near_z:
-        send(buf, (x, z, c, low), ("az", dz), to_z(dz))
+        send(buf, (x, z, c, low), "plane", ("az", dz), to_z(dz))
     for dx in near_x:
-        send(buf, (x, z, c, high), ("bx", dx), to_x(dx))
+        send(buf, (x, z, c, high), "plane", ("bx", dx), to_x(dx))
     for dx in near_x:
-        send(buf, (x, z, c, low), ("ax", 0, dx), to_x(dx))
-    for dz in near_z:
-        send(buf, (x, z, c, high), ("bz", 0, dz), to_z(dz))
-    send(buf, (x, z, c), ("own",), mate)
+        send(buf, (x, z, c, low), "plane", ("ax", 0), to_x(dx))
+    for dz in far_z:
+        send(buf, (x, z, c, high), "plane", ("bz", dz), to_z(dz))
+    send(buf, (x, z, c), "mate", "mate", mate)
 
     loads["step"].wait()
     loads["rate"].wait()
@@ -197,7 +192,7 @@
     total = -rate[:, 0:1] * jnp.sum(step, axis=1, keepdims=True)
     dec[x, z, c] = jnp.sum(jnp.where(rows8 == lanes8, total, 0.0), axis=0, keepdims=True)
     for dz in near_z:
-        send(dec, (x, z, c), ("dz", dz), to_z(dz))
+        send(dec, (x, z, c), "dz", "dz", to_z(dz))
 
     s_index = lax.broadcasted_iota(jnp.int32, (TOK, TOK), 0)
     t_index = lax.broadcasted_iota(jnp.int32, (TOK, TOK), 1)
@@ -229,8 +224,12 @@
         dy_wide = dir_ref[:, span].astype(F32) * columns[:, 24:25]
         dy_pair = dy_wide.astype(BF16)
         dir_ref[:, span] = dy_pair
-        xf_ref[:, span] = (x_wide * pair_columns(columns, 16, pair, low_half)).astype(BF16)
-        dyg_ref[:, span] = (dy_wide * pair_columns(columns, 8, pair, low_half)).astype(BF16)
+        scaled = (x_wide * pair_columns(columns, 16, pair, low_half)).astype(BF16)
+        xf_ref[:, span] = scaled
+        xf_t[span] = scaled.T
+        scaled = (dy_wide * pair_columns(columns, 8, pair, low_half)).astype(BF16)
+        dyg_ref[:, span] = scaled
+        dyg_t[span] = scaled.T
         overlap.append(jnp.sum(x_wide * dy_wide, axis=0, keepdims=True))
         for h in (2 * pair, 2 * pair + 1):
             half = slice(HEADDIM * (h % 2), HEADDIM * (h % 2) + HEADDIM)
@@ -244,26 +243,34 @@
     def forward_low(dz):
         where = (x, from_z(dz), c, low)
         arrive(buf, where, ("az", dz))
-        for dx in near_x:
-            send(buf, where, ("ax", dz, dx), to_x(dx))
-        send(buf, where, ("am", dz), mate)
+        for dx in far_x:
+            send(buf, where, "plane", ("ax", dz), to_x(dx))
+        send(buf, where, "mate", "mate", mate)
 
     def forward_high(dx):
         where = (from_x(dx), z, c, high)
         arrive(buf, where, ("bx", dx))
-        for dz in near_z:
-            send(buf, where, ("bz", dx, dz), to_z(dz))
-        send(buf, where, ("bm", dx), mate)
-
-    def take_low(dz, dx):
-        where = (from_x(dx), from_z(dz), c, low)
-        arrive(buf, where, ("ax", dz, dx))
-        send(buf, where, ("axm", dz, dx), mate)
+        for dz in far_z:
+            send(buf, where, "plane", ("bz", dz), to_z(dz))
+        send(buf, where, "mate", "mate", mate)
+
+    def take_low(dz):
+        zz = from_z(dz)
+        arrive(buf, (pl.ds(0, NX - 1), zz, c, low), ("ax", dz))
+        for dx in near_x:
+            send(buf, (from_x(dx), zz, c, low), "mate", "mate", mate)
 
     def take_high(dz):
-        for dx in (0, 1, 3, 2):
-            arrive(buf, (from_x(dx), from_z(dz), c, high), ("bz", dx, dz))
-        send(buf, (every, from_z(dz), c, high), ("bzm", dz), mate)
+        where = (every, from_z(dz), c, high)
+        arrive(buf, where, ("bz", dz))
+        send(buf, where, "mate", "mate", mate)
+
+    def turn(group):
+        if group == 0:
+            loads["hid"].wait()
+        for j in range(4 * group, 4 * group + 4):
+            span = slice(NC * DEPTH * j, NC * DEPTH * (j + 1))
+            hid_t[span] = hid[:, span].T
 
     prepare(0)
     for dz in (1, 7):
@@ -277,56 +284,42 @@
     prepare(2)
     for dz in (3, 5, 4):
         forward_low(dz)
-    for dz in near_z:
-        arrive(dec, (x, from_z(dz), c), ("dz", dz))
+    arrive(dec, (x, pl.ds(0, NZ - 1), c), "dz")
     for dx in near_x:
-        send(dec, (x, every, c), ("dx", dx), to_x(dx))
+        send(dec, (x, every, c), "dx", "dx", to_x(dx))
     prepare(3)
-    for dx in near_x:
-        take_low(0, dx)
+    for group in range(5):
+        turn(group)
+    take_low(0)
     for dz in (1, 7):
-        for dx in near_x:
-            take_low(dz, dx)
-    for dz in (1, 7):
+        take_low(dz)
+    for dz in (2, 6):
+        take_low(dz)
+    for dz in (1, 7, 2, 6):
         take_high(dz)
-    for dz in (2, 6):
-        for dx in near_x:
-            take_low(dz, dx)
-    for dz in (2, 6):
+    for group in range(5, 8):
+        turn(group)
+    arrive(dec, (pl.ds(0, NX - 1), every, c), "dx")
+    send(dec, (every, every, c), "dm", "dm", mate)
+    for dz in (3, 5, 4):
+        take_low(dz)
         take_high(dz)
-    for dx in near_x:
-        arrive(dec, (from_x(dx), every, c), ("dx", dx))
-    send(dec, (every, every, c), ("dm",), mate)
-    for dz in (3, 5, 4):
-        for dx in near_x:
-            take_low(dz, dx)
-        take_high(dz)
 
     other = 1 - c
-    arrive(buf, (x, z, other), ("own",))
-    for dz in near_z:
-        arrive(buf, (x, from_z(dz), other, low), ("am", dz))
-    for dx in near_x:
-        arrive(buf, (from_x(dx), z, other, high), ("bm", dx))
-    for dz in (0,) + near_z:
-        for dx in near_x:
-            arrive(buf, (from_x(dx), from_z(dz), other, low), ("axm", dz, dx))
-    for dz in near_z:
-        arrive(buf, (every, from_z(dz), other, high), ("bzm", dz))
-    loads["hid"].wait()
+    arrive(buf, (every, every, other), "mate")
     span = MODEL // NX
     sums = jnp.zeros((TOK, COLS), F32)
     for k in range(NX):
         sums = sums + dot(hid[:, k * span : (k + 1) * span], buf[k].reshape(span, COLS))
     bc = sums.astype(BF16)
     b_in, c_in = bc[:, :NSTATE], bc[:, NSTATE:]
-    lg[0] = dot(xf_ref[...], b_in, ((0,), (0,))).reshape(2, WIDE // 2, NSTATE)
-    lg[1] = dot(dyg_ref[...], c_in, ((0,), (0,))).reshape(2, WIDE // 2, NSTATE)
-    send(lg, (every, other), ("l1",), mate, mate_lg)
-    send(lg, (every, c), ("l2",), mate, mate_lg)
+    lg[0] = dot(xf_t[...], b_in).reshape(2, WIDE // 2, NSTATE)
+    lg[1] = dot(dyg_t[...], c_in).reshape(2, WIDE // 2, NSTATE)
+    send(lg, (every, other), "lg", "l1", mate, mate_lg)
+    send(lg, (every, c), "lg", "l2", mate, mate_lg)
 
     starts = sequence_starts(stretch_ref)
-    arrive(dec, (every, every, other), ("dm",))
+    arrive(dec, (every, every, other), "dm")
     row0, row1 = jnp.exp(dec[x, z, 0]), jnp.exp(dec[x, z, 1])
     lane1 = lax.broadcasted_iota(jnp.int32, (1, 128), 1)
 
@@ -336,7 +329,7 @@
     keep0, keep1 = keep_of(2 * chip, starts), keep_of(2 * chip + 1, starts)
     next1 = jnp.where(2 * chip + 2 == NCTX, 0.0, keep_of(2 * chip + 2, starts))
     first = c == 0
-    arrive(mate_lg, (every, c), ("l1",))
+    arrive(mate_lg, (every, c), "l1")
     met = jnp.zeros((HEADDIM, 128), F32)
     chip_l, chip_g = [], []
     for hh in range(HEADS // 2):
@@ -400,7 +393,8 @@
     wide_row = lax.broadcasted_iota(jnp.int32, (WIDE, 128), 0) // HEADDIM
     wide_lane = lax.broadcasted_iota(jnp.int32, (WIDE, 128), 1)
     overlap_row = jnp.broadcast_to(jnp.concatenate(overlap, axis=1), (8, WIDE))
-    overlap_head = dot(overlap_row, (wide_row == wide_lane).astype(F32), precision=lax.Precision.HIGHEST)
+    overlap_head = dot(overlap_row, ((wide_row == wide_lane) | (wide_row == wide_lane - HEADS)).astype(F32), precision=lax.Precision.HIGHEST)
+    skip_grads = overlap_head[1:2]
     skip_row = jnp.zeros((1, 128), F32)
     for h in range(HEADS):
         skip_row = jnp.where(lane1 == h, skip_ref[h], skip_row)
@@ -468,20 +462,20 @@
     gathered = jnp.sum(near[...], axis=0)
     part[1] = gathered
 
-    def spread_head(k, carry):
-        to = (head + k // 2) % NHEAD
-        who = chip * 2 + (c + k) % 2
+    for k in HEADS_FAR_FIRST:
         pltpu.make_async_remote_copy(
-            part.at[1], across.at[k], gs.at[1], gr.at[1], device_id=(who, to), device_id_type=MESH
+            part.at[1],
+            across.at[k],
+            gs.at[1],
+            gr.at[1],
+            device_id=(chip * 2 + (c + k) % 2, (head + k // 2) % NHEAD),
+            device_id_type=MESH,
         ).start()
-        return carry
-
-    lax.fori_loop(1, 2 * NHEAD, spread_head, 0)
     across[0] = gathered
 
     settle(states.at[c], recv_sem.at[1])
-    send(states, (c,), ("st",), mate)
-    arrive(mate_lg, (every, other), ("l2",))
+    send(states, (c,), "st", "st", mate)
+    arrive(mate_lg, (every, other), "l2")
 
     def spaced(row):
         return jnp.concatenate(
@@ -492,53 +486,59 @@
     lead_mate = jnp.where(first, 0.0, keep1)
     trail = jnp.where(first, next1 * keep1 * spaced(row1), next1)
     trail_mate = jnp.where(first, keep1, 0.0)
-    arrive(states, (other,), ("st",))
+    arrive(states, (other,), "st")
     states_f = states[...].astype(F32)
     state_in = lead * states_f[:, :, 0:8].reshape(WIDE, NSTATE)
     state_in = state_in + lead_mate * mate_lg[0].reshape(WIDE, NSTATE)
     grad_state = trail * states_f[:, :, 8:16].reshape(WIDE, NSTATE)
     grad_state = grad_state + trail_mate * mate_lg[1].reshape(WIDE, NSTATE)
 
-    columns = cols_ref[...]
     state_bf, gstate_bf = state_in.astype(BF16), grad_state.astype(BF16)
-    pick_half = lanes8 // HEADDIM
-    nt = ((1,), (1,))
-    carried = jnp.zeros((8, TOK), F32)
-    kept = jnp.zeros((8, TOK), F32)
-    for pair in range(HEADS // 2):
-        span = slice(128 * pair, 128 * pair + 128)
-        picks = (rows8 == 2 * pair + pick_half).astype(BF16)
-        top, rest = halves(dot(c_in, state_bf[span], nt) * dyg_ref[:, span].astype(F32))
-        carried = carried + dot(picks, top, nt) + dot(picks, rest, nt)
-        pulled = dot(b_in, gstate_bf[span], nt) * pair_columns(columns, 16, pair, low_half)
-        top, rest = halves(pulled * x_ref[:, span].astype(F32))
-        kept = kept + dot(picks, top, nt) + dot(picks, rest, nt)
-        gx_ref[:, span] = gx_ref[:, span] + pulled
-    gcols_ref[:, :NSTATE] = gcols_ref[:, :NSTATE] + dot(xf_ref[...], gstate_bf)
-    gcols_ref[:, NSTATE:] = gcols_ref[:, NSTATE:] + dot(dyg_ref[...], state_bf)
-
-    grad_decay = jnp.sum(
-        jnp.sum((state_in * grad_state).reshape(HEADS, HEADDIM, NSTATE), axis=1), axis=1, keepdims=True
-    )
-    end = jnp.sum(kept, axis=1, keepdims=True) + grad_decay * jnp.exp(last)
-    token = lax.broadcasted_iota(jnp.int32, (8, TOK), 1)
-    grad_cum = drow[...] - dcol[...] + carried - kept + jnp.where(token == TOK - 1, end, 0.0)
-    tail = dot(grad_cum, (s_index >= t_index).astype(F32), precision=lax.Precision.HIGHEST)
-    grad_step = (dcol[...] + kept) / step - rate * tail
-    grad_rate = -jnp.sum(step * tail, axis=1, keepdims=True)
-    rate_row = jnp.sum(jnp.where(lanes8 == rows8, grad_rate, 0.0), axis=0, keepdims=True)
-
-    grads = gcols_ref[...].astype(BF16)
+    grads = jnp.concatenate(
+        [
+            gcols_ref[:, :NSTATE] + dot(xf_ref[...], gstate_bf),
+            gcols_ref[:, NSTATE:] + dot(dyg_ref[...], state_bf),
+        ],
+        axis=1,
+    ).astype(BF16)
+
+    def token_grads():
+        columns = cols_ref[...]
+        pick_half = lanes8 // HEADDIM
+        nt = ((1,), (1,))
+        carried = jnp.zeros((8, TOK), F32)
+        kept = jnp.zeros((8, TOK), F32)
+        for pair in range(HEADS // 2):
+            span = slice(128 * pair, 128 * pair + 128)
+            picks = (rows8 == 2 * pair + pick_half).astype(BF16)
+            top, rest = halves(dot(c_in, state_bf[span], nt) * dyg_ref[:, span].astype(F32))
+            carried = carried + dot(picks, top, nt) + dot(picks, rest, nt)
+            pulled = dot(b_in, gstate_bf[span], nt) * pair_columns(columns, 16, pair, low_half)
+            top, rest = halves(pulled * x_ref[:, span].astype(F32))
+            kept = kept + dot(picks, top, nt) + dot(picks, rest, nt)
+            gx_ref[:, span] = gx_ref[:, span] + pulled
+        grad_decay = jnp.sum(
+            jnp.sum((state_in * grad_state).reshape(HEADS, HEADDIM, NSTATE), axis=1), axis=1, keepdims=True
+        )
+        end = jnp.sum(kept, axis=1, keepdims=True) + grad_decay * jnp.exp(last)
+        token = lax.broadcasted_iota(jnp.int32, (8, TOK), 1)
+        grad_cum = drow[...] - dcol[...] + carried - kept + jnp.where(token == TOK - 1, end, 0.0)
+        tail = dot(grad_cum, (s_index >= t_index).astype(F32), precision=lax.Precision.HIGHEST)
+        gstep_ref[...] = (dcol[...] + kept) / step - rate * tail
+        grad_rate = -jnp.sum(step * tail, axis=1, keepdims=True)
+        rate_row = jnp.sum(jnp.where(lanes8 == rows8, grad_rate, 0.0), axis=0, keepdims=True)
+        few[0] = jnp.where(lane1 < HEADS, rate_row, skip_grads)
+
     order = (4, 3, 5, 2, 6, 1, 7, 0)
 
     def multiply(k):
         zz = (z + order[k]) % NZ
         for dx in range(NX):
             first_column = (((x + dx) % NX) * NZ + zz) * (NC * DEPTH)
-            chunk = hid[:, pl.ds(pl.multiple_of(first_column, NC * DEPTH), NC * DEPTH)]
-            prod[k, dx] = dot(chunk, grads, ((0,), (0,))).reshape(NC, DEPTH, COLS)
+            chunk = hid_t[pl.ds(pl.multiple_of(first_column, NC * DEPTH), NC * DEPTH)]
+            prod[k, dx] = dot(chunk, grads).reshape(NC, DEPTH, COLS)
             mate_out[k, dx] = prod[k, dx, other].astype(BF16)
-        send(mate_out, (k,), ("m", k), mate, mate_in)
+        send(mate_out, (k,), "m", ("m", k), mate, mate_in)
 
     def scale_of(block, seq_sums):
         one, two, three = starts
@@ -555,90 +555,96 @@
         for dx in (2, 1, 3):
             both = prod[k, dx, c] * scale + mate_in[k, dx].astype(F32) * scale_mate
             a_out[k, dx - 1] = both[:PART].astype(BF16)
-            send(a_out, (k, dx - 1), ("a", k, dx), to_x(dx), a_in)
+            send(a_out, (k, dx - 1), "a", ("a", k), to_x(dx), a_in)
             prod[k, dx, c, PART:] = both[PART:]
         both = prod[k, 0, c] * scale + mate_in[k, 0].astype(F32) * scale_mate
         a_own[k] = both[:PART]
         prod[k, 0, c, PART:] = both[PART:]
         if dz:
             b_out[k] = prod[k, :, c, PART:].astype(BF16)
-            send(b_out, (k,), ("b", k), to_z(dz), bz_in)
+            send(b_out, (k,), "b", "b", to_z(dz), bz_in)
 
     def pass_on(k):
         dz = order[k]
-        for dx in (1, 2, 3):
-            arrive(a_in, (k, dx - 1), ("a", k, dx))
+        arrive(a_in, (k,), ("a", k))
         a_own[k] = a_own[k] + jnp.sum(a_in[k].astype(F32), axis=0)
         if dz:
             a2_out[k] = a_own[k].astype(BF16)
-            send(a2_out, (k,), ("a2", k), to_z(dz), a2_in)
+            send(a2_out, (k,), "a2", "a2", to_z(dz), a2_in)
 
     for k in range(AHEAD):
         multiply(k)
+    token_grads()
     settle_few(across, gr.at[1], 2 * NHEAD - 1)
     seq_sums = jnp.sum(across[...], axis=0)
     scale, scale_mate = scale_of(index, seq_sums), scale_of(index + 1 - 2 * c, seq_sums)
+    few[0] = few[0] * scale
+    move(few.at[0], few_c, "fc", "fc", mate)
     for k in range(NZ):
         combine(k)
+        if k == 1:
+            arrive(few_c, (every,), "fc")
+            few[1] = few[0] + few_c[...]
+            for j, (dx, dz) in enumerate(FAR_FIRST):
+                move(few.at[1], few_all.at[j], "fz", "fz", at(x + dx, z + dz, c, head))
         if k + AHEAD < NZ:
             multiply(k + AHEAD)
 
-    few[0] = jnp.where(rows8 == 0, rate_row, overlap_head) * scale
-    send(few, (0,), ("fc",), mate, few_c)
     gx_bf[...] = (gx_ref[...] * scale).astype(BF16)
-    gstep_ref[...] = grad_step * scale
+    gstep_ref[...] = gstep_ref[...] * scale
     stores = [
         pltpu.make_async_copy(gx_bf, grad_x_out, load_sem.at[0]),
         pltpu.make_async_copy(gstep_ref, grad_step_out, load_sem.at[1]),
     ]
     for store in stores:
         store.start()
-    arrive(few_c, (0,), ("fc",))
-    few[1] = few[0] + few_c[0]
-
     pass_on(0)
-    for dz in near_z:
-        send_few(1, few_z, dz - 1, ("fz", dz), to_z(dz))
     for k in range(1, 4):
         pass_on(k)
-    for dz in near_z:
-        arrive(few_z, (dz - 1,), ("fz", dz))
-    few[2] = few[1] + jnp.sum(few_z[...], axis=0)
-    for dx in near_x:
-        send_few(2, few_x, dx - 1, ("fx", dx), to_x(dx))
     pass_on(4)
     b_sum = prod[NZ - 1, :, c, PART:]
+    arrive(bz_in, (every,), "b")
     for k in range(NZ - 1):
-        arrive(bz_in, (k,), ("b", k))
         b_sum = b_sum + bz_in[k].astype(F32)
     for dx in (2, 1, 3):
         b2_out[dx - 1] = b_sum[dx].astype(BF16)
-        send(b2_out, (dx - 1,), ("b2", dx), to_x(dx), b2_in)
+        send(b2_out, (dx - 1,), "b2", "b2", to_x(dx), b2_in)
     for k in range(5, NZ):
         pass_on(k)
-    for dx in near_x:
-        arrive(few_x, (dx - 1,), ("fx", dx))
-    small[...] = few[2] + jnp.sum(few_x[...], axis=0)
+    arrive(b2_in, (every,), "b2")
+    gw_ref[PART:] = b_sum[0] + jnp.sum(b2_in[...].astype(F32), axis=0)
+    a_sum = a_own[NZ - 1]
+    arrive(few_all, (every,), "fz")
+    small = few[1] + jnp.sum(few_all[...], axis=0)
     for h in range(HEADS):
         rate_ref[h] = small[0, h]
-        skip_ref[h] = small[1, h]
+        skip_ref[h] = small[0, HEADS + h]
     stores.append(pltpu.make_async_copy(rate_ref, rate_out, load_sem.at[2]))
     stores.append(pltpu.make_async_copy(skip_ref, skip_out, load_sem.at[4]))
     stores[-2].start()
     stores[-1].start()
-    for dx in near_x:
-        arrive(b2_in, (dx - 1,), ("b2", dx))
-    gw_ref[PART:] = b_sum[0] + jnp.sum(b2_in[...].astype(F32), axis=0)
-    a_sum = a_own[NZ - 1]
+    arrive(a2_in, (every,), "a2")
     for k in range(NZ - 1):
-        arrive(a2_in, (k,), ("a2", k))
         a_sum = a_sum + a2_in[k].astype(F32)
     gw_ref[:PART] = a_sum
     stores.append(pltpu.make_async_copy(gw_ref, grad_w_out, load_sem.at[3]))
     stores[-1].start()
 
-    for copy in started:
-        copy.wait_send()
+    drain("plane", moves.at[pl.ds(0, NZ // 2), pl.ds(0, TOK - 8)])
+    drain("mate", buf.at[:, :, c])
+    drain("dz", dec.at[x, pl.ds(0, NZ - 1), c])
+    drain("dx", dec.at[pl.ds(0, NX - 1), :, c])
+    drain("dm", dec.at[:, :, c])
+    drain("lg", lg)
+    drain("st", states.at[c])
+    drain("m", mate_out)
+    drain("a", a_out)
+    drain("b", b_out)
+    drain("a2", a2_out)
+    drain("b2", b2_out)
+    drain("fc", few.at[0])
+    drain("fz", few_all)
+    assert not sent
     settle(msg, send_sem.at[0])
     settle(reply, send_sem.at[1])
     settle_few(near, gs.at[0], CHIPS - 1)
@@ -650,7 +656,6 @@
 def whole(hidden, w_bc, x_act, logp_dir, step_size, rate, skip, mask, base, stretches):
     shape = jax.ShapeDtypeStruct
     rest = DEPTH - PART
-    count = 190
     return pl.pallas_call(
         whole_kernel,
         name="whole",
@@ -695,12 +700,14 @@
             pltpu.VMEM((2, 1, 128), F32),
             pltpu.VMEM((CHIPS, 1, 128), F32),
             pltpu.VMEM((2 * NHEAD, 1, 128), F32),
+            pltpu.VMEM((MODEL, TOK), BF16),
+            pltpu.VMEM((WIDE, TOK), BF16),
+            pltpu.VMEM((WIDE, TOK), BF16),
             pltpu.VMEM((TOK, WIDE), F32),
             pltpu.VMEM((TOK, COLS), F32),
             pltpu.VMEM((TOK, WIDE), BF16),
             pltpu.VMEM((8, TOK), F32),
             pltpu.VMEM((DEPTH, COLS), F32),
-            pltpu.VMEM((8, 128), F32),
             pltpu.VMEM((NZ, NX, NC, DEPTH, COLS), F32),
             pltpu.VMEM((NZ, NX, DEPTH, COLS), BF16),
             pltpu.VMEM((NZ, NX, DEPTH, COLS), BF16),
@@ -713,15 +720,14 @@
             pltpu.VMEM((NZ - 1, NX, rest, COLS), BF16),
             pltpu.VMEM((NX - 1, rest, COLS), BF16),
             pltpu.VMEM((NX - 1, rest, COLS), BF16),
-            pltpu.VMEM((3, 8, 128), F32),
-            pltpu.VMEM((1, 8, 128), F32),
-            pltpu.VMEM((NZ - 1, 8, 128), F32),
-            pltpu.VMEM((NX - 1, 8, 128), F32),
+            pltpu.VMEM((2, 1, 128), F32),
+            pltpu.VMEM((1, 128), F32),
+            pltpu.VMEM((CHIPS - 1, 1, 128), F32),
             pltpu.SemaphoreType.DMA((10,)),
             pltpu.SemaphoreType.DMA((2,)),
             pltpu.SemaphoreType.DMA((2,)),
-            pltpu.SemaphoreType.DMA((count,)),
-            pltpu.SemaphoreType.DMA((count,)),
+            pltpu.SemaphoreType.DMA((14,)),
+            pltpu.SemaphoreType.DMA((53,)),
             pltpu.SemaphoreType.DMA((2,)),
             pltpu.SemaphoreType.DMA((2,)),
         ],

time: 71.4 us -> 67.8 us (0.950)
  Pallas kernels: 70.1 us -> 67 us
    pallas_call x1, Pallas kernels: 68.3 us -> 65.3 us  [whole(): pl.pallas_call(whole_kernel, name='whole', out_shape=(shape((TOK, WIDE),...]
where the time goes in v4:
time: 67.8 us; the launch traced here: 67.7 us
  Pallas kernels  67 us (99%)
    pallas_call x1, Pallas kernels, whole(): pl.pallas_call(whole_kernel, name='whole', out_shape=(shape((TOK, WIDE),...  65.3 us
    pallas_call x1, Pallas kernels, finish(): pl.pallas_call(finish_kernel, name='finish', out_shape=tuple((jax.ShapeDt...  1.77 us

profile of v4, /device:TPU:1, one launch (start us, length us, event | category | flops | bytes accessed | tf_op | source)
XLA Modules:
  0.0 67.7 jit_solution(6953255104228092527)
XLA Ops:
  0.6 65.3 %whole.1 = (bf16[256,512]{1,0:T(8,128)(2,1)}, f32[8,256]{1,0:T(8,128)}, f32[8]{0:T(128)}, f32[8]{0:T(128)}, f32[64,256]{1,0:T(8,128)}) custom-call(bf16[256,4096]{1,0:T(8,128)(2,1)} %hid_hbm.1, bf16[64,256]{1,0:T(8,128)(2,1)} %w_hbm.1, bf16[256,512]{1,0:T(8,128)(2,1)} %x_hbm.1, bf16[256,512]{1,0:T(8,128)(2,1)} %dir_hbm.1, f32[8,256]{1,0:T(8,128)} %step_hbm.1, ...), custom_call_target="tpu_custom_call" | custom-call | tf_op jit(solution)/shard_map/whole/pallas_call | solution.py:659
  65.9 1.8 %finish.1 = (bf16[256,512]{1,0:T(8,128)(2,1)}, f32[8,256]{1,0:T(8,128)}, f32[8]{0:T(128)}, f32[8]{0:T(128)}, f32[64,256]{1,0:T(8,128)}) custom-call(bf16[256,512]{1,0:T(8,128)(2,1)} %get-tuple-element.10.refs_0_, f32[8,256]{1,0:T(8,128)} %get-tuple-element.11.refs_1_, f32[8]{0:T(128)} %get-tuple-element.12.refs_2_, f32[8]{0:T(128)} %get-tuple-element.13.refs_3_, ...), custom_call_target="tpu_custom_call" | custom-call | tf_op jit(solution)/shard_map/finish/pallas_call | solution.py:757

commit v5 on v4

--- a/solution.py
+++ b/solution.py
@@ -740,14 +740,24 @@
 def finish_kernel(*refs):
     *ends, sems = refs
     count = len(ends) // 3
-    sources, targets, holds = ends[:count], ends[count : 2 * count], ends[2 * count :]
-    into = [pltpu.make_async_copy(sources[k], holds[k], sems.at[k]) for k in range(count)]
-    back = [pltpu.make_async_copy(holds[k], targets[k], sems.at[count + k]) for k in range(count)]
+    steps = []
+    for k in range(count):
+        trio = ends[k], ends[2 * count + k], ends[count + k]
+        rows = trio[0].shape[0]
+        if rows > DEPTH:
+            steps += [[ref.at[pl.ds(first, DEPTH)] for ref in trio] for first in range(0, rows, DEPTH)]
+        else:
+            steps.append(trio)
+    into = [pltpu.make_async_copy(source, hold, sems.at[k]) for k, (source, hold, _) in enumerate(steps)]
+    back = [
+        pltpu.make_async_copy(hold, target, sems.at[len(steps) + k])
+        for k, (_, hold, target) in enumerate(steps)
+    ]
     for copy in into:
         copy.start()
-    for k in reversed(range(count)):
-        into[k].wait()
-        back[k].start()
+    for arrived, copy in zip(into, back):
+        arrived.wait()
+        copy.start()
     for copy in back:
         copy.wait()
 
@@ -763,7 +773,7 @@
         scratch_shapes=[
             (pltpu.VMEM if array.ndim == 2 else pltpu.SMEM)(array.shape, array.dtype) for array in arrays
         ]
-        + [pltpu.SemaphoreType.DMA((2 * len(arrays),))],
+        + [pltpu.SemaphoreType.DMA((2 * sum(max(1, array.shape[0] // DEPTH) for array in arrays),))],
         compiler_params=pltpu.CompilerParams(vmem_limit_bytes=VMEM_LIMIT),
     )(*arrays)
 

time: 67.8 us -> 67.9 us (level)
  no operation moved by 1% of the time
where the time goes in v5:
time: 67.9 us; the launch traced here: 67.7 us
  Pallas kernels  67 us (99%)
    pallas_call x1, Pallas kernels, whole(): pl.pallas_call(whole_kernel, name='whole', out_shape=(shape((TOK, WIDE),...  65.3 us
    pallas_call x1, Pallas kernels, finish(): pl.pallas_call(finish_kernel, name='finish', out_shape=tuple((jax.ShapeDt...  1.75 us

profile of v5, /device:TPU:1, one launch (start us, length us, event | category | flops | bytes accessed | tf_op | source)
XLA Modules:
  0.0 67.7 jit_solution(9903731351886245392)
XLA Ops:
  0.6 65.3 %whole.1 = (bf16[256,512]{1,0:T(8,128)(2,1)}, f32[8,256]{1,0:T(8,128)}, f32[8]{0:T(128)}, f32[8]{0:T(128)}, f32[64,256]{1,0:T(8,128)}) custom-call(bf16[256,4096]{1,0:T(8,128)(2,1)} %hid_hbm.1, bf16[64,256]{1,0:T(8,128)(2,1)} %w_hbm.1, bf16[256,512]{1,0:T(8,128)(2,1)} %x_hbm.1, bf16[256,512]{1,0:T(8,128)(2,1)} %dir_hbm.1, f32[8,256]{1,0:T(8,128)} %step_hbm.1, ...), custom_call_target="tpu_custom_call" | custom-call | tf_op jit(solution)/shard_map/whole/pallas_call | solution.py:659
  65.9 1.8 %finish.1 = (bf16[256,512]{1,0:T(8,128)(2,1)}, f32[8,256]{1,0:T(8,128)}, f32[8]{0:T(128)}, f32[8]{0:T(128)}, f32[64,256]{1,0:T(8,128)}) custom-call(bf16[256,512]{1,0:T(8,128)(2,1)} %get-tuple-element.10.refs_0_, f32[8,256]{1,0:T(8,128)} %get-tuple-element.11.refs_1_, f32[8]{0:T(128)} %get-tuple-element.12.refs_2_, f32[8]{0:T(128)} %get-tuple-element.13.refs_3_, ...), custom_call_target="tpu_custom_call" | custom-call | tf_op jit(solution)/shard_map/finish/pallas_call | solution.py:767
